TPU v7x, 128 devices: a whole 4x4x4 slice. The times are simulated.
128 devices in a mesh: dp: 16 (over z, y), pipe: 2 (over x_hi), tensor: 4 (over x_lo, core).
Axes of the slice: x: 4 (x_hi: 2, x_lo: 2; x = x_hi * 2 + x_lo), y: 4, z: 4, core: 2. Of those that a mesh axis runs over, the one named last changes fastest.
Arguments:
- residual_input: bfloat16 [1024, 8192], P('dp', 'tensor'), may hold values from -6 to 6
- layer_norm_gain: bfloat16 [2, 8192], P('pipe'), may hold values from 0.099609375 to 1.8984375
- query_weight: bfloat16 [2, 8192, 8192], P('pipe', 'dp', 'tensor'), may hold values from -0.0625 to 0.0625
- key_weight: bfloat16 [2, 8192, 1024], P('pipe', 'dp', 'tensor'), may hold values from -0.0625 to 0.0625
- value_weight: bfloat16 [2, 8192, 1024], P('pipe', 'dp', 'tensor'), may hold values from -0.0625 to 0.0625
- output_weight: bfloat16 [2, 8192, 8192], P('pipe', 'tensor', 'dp'), may hold values from -0.0625 to 0.0625
- adapter_down_weight: bfloat16 [2, 8192, 8, 128], P('pipe', 'tensor'), may hold values from -0.0625 to 0.0625
- adapter_up_weight: bfloat16 [2, 8, 128, 8192], P('pipe', None, None, 'tensor'), may hold values from -0.5 to 0.5
- cached_key_rows: bfloat16 [2, 1024, 80, 1024], P('pipe', 'dp', None, 'tensor'), may hold values from -280 to 280
- cached_value_rows: bfloat16 [2, 1024, 80, 1024], P('pipe', 'dp', None, 'tensor'), may hold values from -6 to 6
- request_adapter: int32 [1024], P('dp'), may hold values from 0 to 7
- rank_per_adapter: int32 [8], replicated, may hold values from 16 to 128, as said below
- cached_length: int32 [1024], P('dp'), may hold values from 1 to 80, as said below
Outputs:
- hidden_out: bfloat16 [1024, 8192], P(('dp', 'pipe'), 'tensor')
Inputs may be any that keep to these rules, and one draw needn't show every extreme that they name: `rank_per_adapter`: some adapter has rank exactly 128. `cached_length`: some request has exactly 80 cached positions; a request's new token stands at the position equal to its length.
All inputs are finite; a program needn't handle non-finite values.
Results may differ from a plain program's by a relative error of at most 0.025.
Values may be sent and summed in bfloat16 or wider, within the bound.
No kernel may reach another device: no remote copies, remote signals or barrier semaphores. Data moves between devices by JAX's collectives and lax.ppermute only.
A program may use at most 128 MiB of HBM per device.

v0:
```python
import jax
import jax.numpy as jnp
from jax import lax
from jax.experimental import pallas as pl
from jax.experimental.pallas import tpu as pltpu
from jax.sharding import Mesh
from jax.sharding import PartitionSpec as P

HEAD = 128
RANK = 128
ADAPTERS = 8
CTX = 80
EPS = 1e-05
SCALE = 64.0
LANES = 128
AXES = ("z", "y", "pipe", "xl", "core")
DP = ("z", "y")
RING = ("pipe", "xl")
bf16 = jnp.bfloat16
f32 = jnp.float32


def send(block, route):
    pairs = []
    for z in range(4):
        for y in range(4):
            for p in range(2):
                for xl in range(2):
                    for c in range(2):
                        there = route(z, y, p, xl, c)
                        if there is None:
                            continue
                        source = ((z * 4 + y) * 2 + p) * 4 + xl * 2 + c
                        a, b, q, u, v = there
                        target = (((a % 4) * 4 + b % 4) * 2 + q) * 4 + u * 2 + v
                        pairs.append((source, target))
    return lax.ppermute(block, AXES, pairs)


def other_core(z, y, p, u, c):
    return (z, y, p, u, 1 - c)


def other_xl(z, y, p, u, c):
    return (z, y, p, 1 - u, c)


def other_pipe(z, y, p, u, c):
    return (z, y, 1 - p, u, c)


def pipe_from(source):
    return lambda z, y, p, u, c: (z, y, 1 - p, u, c) if p == source else None


def exchange(blocks, axes):
    return lax.all_to_all(blocks, axes, 0, 0, tiled=True)


def after(value, earlier):
    return lax.optimization_barrier((value, earlier))[0]


def project_in_kernel(with_squares, x_ref, w_ref, out_ref):
    x = x_ref[...]
    width = w_ref.shape[1]
    out_ref[:, :width] = jnp.dot(x, w_ref[...], preferred_element_type=f32).astype(bf16)
    if with_squares:
        x = x.astype(f32)
        total = jnp.sum(x * x, axis=1, keepdims=True)
        high = total.astype(bf16).astype(f32)
        lane = lax.broadcasted_iota(jnp.int32, (x.shape[0], LANES), 1)
        out_ref[:, width:] = jnp.where(lane == 0, high, total - high).astype(bf16)


def project_in(state, weights, with_squares, tile=256):
    rows, depth = state.shape
    width = weights.shape[1]
    wide = width + LANES if with_squares else width
    return pl.pallas_call(
        lambda *refs: project_in_kernel(with_squares, *refs),
        grid=(rows // tile,),
        in_specs=[
            pl.BlockSpec((tile, depth), lambda i: (i, 0)),
            pl.BlockSpec((depth, width), lambda i: (0, 0)),
        ],
        out_specs=pl.BlockSpec((tile, wide), lambda i: (i, 0)),
        out_shape=jax.ShapeDtypeStruct((rows, wide), bf16),
        compiler_params=pltpu.CompilerParams(vmem_limit_bytes=32 * 1024 * 1024),
    )(state, weights)


def project_out_kernel(a_ref, ids_ref, w_ref, up_ref, out_ref):
    depth = w_ref.shape[0]
    total = jnp.dot(a_ref[:, :depth], w_ref[...], preferred_element_type=f32)
    shrunk = a_ref[:, depth:]
    ids = ids_ref[...]
    nothing = jnp.zeros_like(shrunk)
    spread = jnp.concatenate(
        [jnp.where(ids == a, shrunk, nothing) for a in range(ADAPTERS)], axis=1
    )
    total = total + jnp.dot(spread, up_ref[...], preferred_element_type=f32)
    out_ref[...] = total.astype(bf16)


def project_out(load, ids, weights, up, tile=256):
    rows, wide = load.shape
    depth, width = weights.shape
    return pl.pallas_call(
        project_out_kernel,
        grid=(rows // tile,),
        in_specs=[
            pl.BlockSpec((tile, wide), lambda i: (i, 0)),
            pl.BlockSpec((tile, RANK), lambda i: (i, 0)),
            pl.BlockSpec((depth, width), lambda i: (0, 0)),
            pl.BlockSpec((ADAPTERS * RANK, width), lambda i: (0, 0)),
        ],
        out_specs=pl.BlockSpec((tile, width), lambda i: (i, 0)),
        out_shape=jax.ShapeDtypeStruct((rows, width), bf16),
        compiler_params=pltpu.CompilerParams(vmem_limit_bytes=32 * 1024 * 1024),
    )(load, ids, weights, up)


def rope_tables(positions):
    half = HEAD // 2
    inv_freq = jnp.exp(-jnp.log(10000.0) * jnp.arange(half, dtype=f32) * (2.0 / HEAD))
    angles = positions.astype(f32)[:, None] * inv_freq[None, :]
    return (jnp.cos(angles), jnp.sin(angles))


def rotate(features, cosine, sine):
    half = HEAD // 2
    a = features[..., :half]
    b = features[..., half:]
    return jnp.concatenate([a * cosine - b * sine, b * cosine + a * sine], axis=-1)


def attend(query, key_new, value_new, keys, values, lengths):
    rows, groups = key_new.shape[:2]
    inverse = float(HEAD) ** (-0.5)
    query = query.reshape(rows, groups, -1, HEAD)
    keys = keys.reshape(rows, CTX, groups, HEAD)
    values = values.reshape(rows, CTX, groups, HEAD)
    scores = jnp.einsum("rgqd,rcgd->rgqc", query, keys, preferred_element_type=f32) * inverse
    own = jnp.einsum("rgqd,rgd->rgq", query, key_new, preferred_element_type=f32) * inverse
    valid = jnp.arange(CTX, dtype=jnp.int32)[None, :] < lengths[:, None]
    masked = jnp.where(valid[:, None, None, :], scores, -1e30)
    top = jnp.maximum(jnp.max(masked, axis=-1), own)
    raw = jnp.exp(masked - top[..., None])
    own_raw = jnp.exp(own - top)
    total = jnp.sum(raw, axis=-1) + own_raw
    weights = (raw / total[..., None]).astype(bf16)
    own_weight = (own_raw / total).astype(bf16)
    out = jnp.einsum("rgqc,rcgd->rgqd", weights, values, preferred_element_type=f32)
    out = out + own_weight.astype(f32)[..., None] * value_new.astype(f32)[:, :, None, :]
    return out.reshape(rows, -1).astype(bf16)


def on_device(
    residual_input,
    layer_norm_gain,
    query_weight,
    key_weight,
    value_weight,
    output_weight,
    adapter_down_weight,
    adapter_up_weight,
    cached_key_rows,
    cached_value_rows,
    request_adapter,
    rank_per_adapter,
    cached_length,
):
    z, y, p = lax.axis_index("z"), lax.axis_index("y"), lax.axis_index("pipe")
    xl, core = lax.axis_index("xl"), lax.axis_index("core")
    x = 2 * p + xl
    group = residual_input.shape[0]
    half = group // 2
    block = query_weight.shape[1]
    qh = query_weight.shape[2] // 2
    kh = key_weight.shape[2] // 2
    all_rows = 16 * group

    gain = lax.dynamic_slice_in_dim(layer_norm_gain[0], (4 * z + y) * block, block, 0)
    gain = gain.astype(f32)[:, None]

    def in_half(which):
        parts = [
            lax.dynamic_slice_in_dim(query_weight[0], which * qh, qh, 1),
            lax.dynamic_slice_in_dim(key_weight[0], which * kh, kh, 1),
            lax.dynamic_slice_in_dim(value_weight[0], which * kh, kh, 1),
        ]
        return (jnp.concatenate(parts, axis=1).astype(f32) * gain).astype(bf16)

    theirs_in = in_half(1 - p)
    cuts = (0, 176, 352, block)
    in_got = [send(theirs_in[: cuts[1]], other_pipe)]

    numbers = jnp.pad(request_adapter.astype(bf16).reshape(1, group), ((0, 15), (0, block - group)))
    got = [None] * 4
    for k in range(4):
        piece = lax.dynamic_slice_in_dim(residual_input, (y + k) % 4 * block, block, 1)
        got[(4 - k) % 4] = send(
            jnp.concatenate([piece, numbers], axis=0),
            lambda z, y, p, u, c, k=k: (2 * u + c, y + k, p, z // 2, z % 2),
        )
    got = after(got, theirs_in)
    quarter = lax.dynamic_slice_in_dim(jnp.stack(got + got), (4 - y) % 4, 4, 0)
    in_got.append(send(after(theirs_in, in_got[0])[cuts[1] : cuts[2]], other_pipe))
    near = send(after(quarter, in_got[0]), other_xl)
    pair = jnp.stack([jnp.where(xl == 0, quarter, near), jnp.where(xl == 0, near, quarter)])
    in_got.append(send(after(theirs_in, in_got[1])[cuts[2] :], other_pipe))
    far = send(after(pair, in_got[1]), other_core)
    even, odd = jnp.where(core == 0, pair, far), jnp.where(core == 0, far, pair)
    rows = jnp.stack([even[0], odd[0], even[1], odd[1]])
    in_got = jnp.concatenate(in_got, axis=0)
    state = rows[:, :, :group].reshape(all_rows, block)
    ids = rows[:, :, group, :group].reshape(all_rows, 1)
    ids = jnp.broadcast_to(ids, (all_rows, RANK))

    square = residual_input.astype(f32)
    square = jnp.sum(square * square, axis=1).reshape(1, group)
    square = square + send(square, other_xl)
    square = square + send(square, other_core)
    square = square.reshape(group, 1)

    chosen = request_adapter[:, None] == jnp.arange(ADAPTERS, dtype=jnp.int32)[None, :]
    rank = jnp.sum(jnp.where(chosen, rank_per_adapter[None, :], 0), axis=1)
    live = jnp.arange(RANK, dtype=jnp.int32)[None, :] < rank[:, None]
    rank_scale = SCALE / rank.astype(f32)
    cosine, sine = rope_tables(cached_length)
    cosine, sine = cosine[:, None, :], sine[:, None, :]

    up = adapter_up_weight[0].reshape(ADAPTERS * RANK, -1)
    up = lax.dynamic_slice_in_dim(up, y * block, block, 1)
    out_mine = lax.dynamic_slice_in_dim(output_weight[0], p * qh, qh, 0)
    out_theirs = lax.dynamic_slice_in_dim(output_weight[0], (1 - p) * qh, qh, 0)
    out_got = send(after(out_theirs, in_got), other_pipe)

    down = adapter_down_weight[0].reshape(-1, ADAPTERS * RANK)

    mine_in = in_half(p)
    for layer in range(2):
        weights = jnp.where(p == layer, mine_in, in_got)
        parts = project_in(state, weights, layer == 1)
        parts = exchange(parts.reshape(16, group, -1), DP)
        if layer == 0:
            parts, out_got = lax.optimization_barrier((parts, out_got))
            up = send(after(up, parts), lambda z, y, p, u, c: (2 * u + c, y, p, z // 2, z % 2))
        ours = jnp.sum(parts.astype(f32), axis=0)
        if layer == 1:
            square = ours[:, qh + 2 * kh : qh + 2 * kh + 1] + ours[:, qh + 2 * kh + 1 : qh + 2 * kh + 2]
        ours = ours[:, : qh + 2 * kh].astype(bf16)
        across = send(ours, pipe_from(1 - layer))
        halves = [ours, across] if layer == 0 else [across, ours]
        features = 4.0 * residual_input.shape[1]
        factor = lax.rsqrt(square / features + EPS)
        halves = [part.astype(f32) * factor for part in halves]
        query = jnp.concatenate([part[:, :qh] for part in halves], axis=1)
        key_new = jnp.concatenate([part[:, qh : qh + kh] for part in halves], axis=1)
        value_new = jnp.concatenate([part[:, qh + kh : qh + 2 * kh] for part in halves], axis=1)
        query = rotate(query.reshape(group, -1, HEAD), cosine, sine).astype(bf16)
        key_new = rotate(key_new.reshape(group, -1, HEAD), cosine, sine).astype(bf16)
        value_new = value_new.reshape(group, -1, HEAD).astype(bf16)
        attended = attend(
            query, key_new, value_new, cached_key_rows[0], cached_value_rows[0], cached_length
        )

        keep = attended[:, layer * qh : (layer + 1) * qh]
        give = attended[:, (1 - layer) * qh : (2 - layer) * qh]
        mine = jnp.where(p == layer, keep, send(give, pipe_from(layer)))
        product = jnp.dot(attended, down, preferred_element_type=f32)
        product = product.reshape(group, ADAPTERS, RANK)
        shrunk = jnp.sum(jnp.where(chosen[:, :, None], product, 0.0), axis=1)
        shrunk = jnp.where(live, shrunk, 0.0) * rank_scale[:, None]
        shrunk = jnp.where(p == layer, shrunk, 0.0)
        load = jnp.concatenate([mine, shrunk.astype(bf16)], axis=1)
        load, up = lax.optimization_barrier((load, up))
        load = exchange(jnp.broadcast_to(load[None], (16,) + load.shape), DP)
        w_out = jnp.where(p == layer, out_mine, out_got)
        partial = project_out(load.reshape(all_rows, -1), ids, w_out, up)

        if layer == 0:
            partial = partial.reshape(2, all_rows // 2, block)
            before = lax.dynamic_index_in_dim(
                state.reshape(8, all_rows // 8, block), core * 4 + x, 0, keepdims=False
            )
        else:
            partial = partial.reshape(16, 2, half, block).transpose(1, 0, 2, 3)
            before = lax.dynamic_index_in_dim(
                state.reshape(4, 4, 2, half, block), x, 0, keepdims=False
            )
            before = lax.dynamic_index_in_dim(before, core, 1, keepdims=False)
        keep = lax.dynamic_index_in_dim(partial, core, 0, keepdims=False)
        give = lax.dynamic_index_in_dim(partial, 1 - core, 0, keepdims=False)
        summed = keep.astype(f32) + send(give, other_core).astype(f32)
        summed = summed.astype(bf16).reshape(4, -1, block)
        summed = exchange(summed, RING)
        total = jnp.sum(summed.astype(f32), axis=0) + before.reshape(-1, block).astype(f32)
        total = total.astype(bf16)
        if layer == 0:
            total = exchange(jnp.broadcast_to(total[None], (4,) + total.shape), RING)
            total = total.reshape(all_rows // 2, block)
            there = send(total, other_core)
            state = jnp.concatenate(
                [jnp.where(core == 0, total, there), jnp.where(core == 0, there, total)], axis=0
            )
        else:
            total = total.reshape(4, half, block)
            pieces = [None] * 4
            for k in range(4):
                piece = lax.dynamic_index_in_dim(total, (y + k) % 4, 0, keepdims=False)
                pieces[(4 - k) % 4] = send(
                    piece, lambda z, y, p, u, c, k=k: (2 * p + u, y + k, c, z // 2, z % 2)
                )
            pieces = lax.dynamic_slice_in_dim(jnp.stack(pieces + pieces), (4 - y) % 4, 4, 0)
            return pieces.transpose(1, 0, 2).reshape(half, 4 * block)


def solution(mesh):
    torus = Mesh(mesh.devices.reshape(4, 4, 2, 2, 2), AXES)
    heads = ("xl", "core")
    placed = (
        P(DP, heads),
        P("pipe", None),
        P("pipe", DP, heads),
        P("pipe", DP, heads),
        P("pipe", DP, heads),
        P("pipe", heads, DP),
        P("pipe", heads, None, None),
        P("pipe", None, None, heads),
        P("pipe", DP, None, heads),
        P("pipe", DP, None, heads),
        P(DP),
        P(),
        P(DP),
    )
    return jax.shard_map(
        on_device,
        mesh=torus,
        in_specs=placed,
        out_specs=P(("z", "y", "pipe"), heads),
        check_vma=False,
    )
```

profile of v0, /device:TPU:1, one launch (start us, length us, event | category | flops | bytes accessed | tf_op | source)
XLA Modules:
  0.0 357.8 jit_solution(15733188183330053651)
XLA Ops:
  2.4 4.0 %collective-permute-start.3 = (bf16[80,512]{1,0:T(8,128)(2,1)}, bf16[80,512]{1,0:T(8,128)(2,1)S(1)}, u32[]{:S(2)}, u32[]{:S(2)}) collective-permute-start(bf16[80,512]{1,0:T(8,128)(2,1)} %get-tuple-element.83), channel_id=1, source_target_pairs={{0,8},{1,40},{2,72},{3,104},{4,12},{5,44},{6,76},{7,108},{8,16},{9... | collective-permute-start | bytes 245768 | tf_op jit(solution)/shard_map/ppermute | solution.py:37
  20.9 7.7 %collective-permute-done.4 = bf16[176,1280]{1,0:T(8,128)(2,1)} collective-permute-done((bf16[176,1280]{1,0:T(8,128)(2,1)}, bf16[176,1280]{1,0:T(8,128)(2,1)}, u32[]{:S(2)}, u32[]{:S(2)}) %collective-permute-start.4) | collective-permute-done | bytes 450592 | tf_op jit(solution)/shard_map/ppermute | solution.py:37
  32.9 5.1 %collective-permute-start.5 = (bf16[4,80,512]{2,1,0:T(8,128)(2,1)}, bf16[4,80,512]{2,1,0:T(8,128)(2,1)}, u32[]{:S(2)}, u32[]{:S(2)}) collective-permute-start(bf16[4,80,512]{2,1,0:T(8,128)(2,1)} %constant_dynamic-slice_fusion.1), channel_id=1, source_target_pairs={{0,2},{1,3},{2,0},{3,1},{4,6},{5,7},{6,4},{7,5},{8,10},{9,11},{10,... | collective-permute-start | bytes 983048 | tf_op jit(solution)/shard_map/ppermute | solution.py:37
  46.1 6.8 %collective-permute-done.5 = bf16[4,80,512]{2,1,0:T(8,128)(2,1)} collective-permute-done((bf16[4,80,512]{2,1,0:T(8,128)(2,1)}, bf16[4,80,512]{2,1,0:T(8,128)(2,1)}, u32[]{:S(2)}, u32[]{:S(2)}) %collective-permute-start.5) | collective-permute-done | bytes 327712 | tf_op jit(solution)/shard_map/ppermute | solution.py:37
  54.0 5.5 %collective-permute-start.7 = (bf16[2,4,80,512]{3,2,1,0:T(8,128)(2,1)S(1)}, bf16[2,4,80,512]{3,2,1,0:T(8,128)(2,1)S(1)}, u32[]{:S(2)}, u32[]{:S(2)}) collective-permute-start(bf16[2,4,80,512]{3,2,1,0:T(8,128)(2,1)S(1)} %pad_maximum_fusion.2), channel_id=1, source_target_pairs={{0,1},{1,0},{2,3},{3,2},{4,5},{5,4},{6,7},{7,6},{8,9},{9,8},{10,11... | collective-permute-start | bytes 1966088 | tf_op jit(solution)/shard_map/ppermute | solution.py:37
  66.9 7.5 %all-to-all-start = ((bf16[16,64,1280]{2,1,0:T(8,128)(2,1)}), bf16[16,64,1280]{2,1,0:T(8,128)(2,1)}, u32[]{:S(2)}, u32[]{:S(2)}) async-start(bf16[16,64,1280]{2,1,0:T(8,128)(2,1)} %bitcast.15), calls=%async_computation | async-start | bytes 5242880 | tf_op jit(solution)/shard_map/all_to_all | solution.py:57
  78.5 4.9 %reshape_squeeze.15 = bf16[64,80,2,128]{3,2,1,0:T(2,128)(2,1)} reshape(bf16[1,64,80,256]{3,2,1,0:T(8,128)(2,1)} %param.21) | data formatting | bytes 5242880 | tf_op jit(solution)/shard_map/reshape;squeeze | solution.py:142
  83.4 4.9 %reshape_squeeze.16 = bf16[64,80,2,128]{3,2,1,0:T(2,128)(2,1)} reshape(bf16[1,64,80,256]{3,2,1,0:T(8,128)(2,1)} %param.22) | data formatting | bytes 5242880 | tf_op jit(solution)/shard_map/reshape;squeeze | solution.py:143
  90.9 5.3 %copy.133 = bf16[256,8,8,128]{3,1,2,0:T(8,128)(2,1)} copy(bf16[256,8,8,128]{3,2,1,0:T(8,128)(2,1)} %bitcast.197) | data formatting | bytes 8388608
  96.2 6.6 %copy.79 = bf16[1024,2048]{1,0:T(8,128)(2,1)} copy(bf16[1024,2048]{0,1:T(8,128)(2,1)} %bitcast.194) | data formatting | bytes 8388608 | tf_op jit(solution)/shard_map/dot_general | solution.py:272
  110.5 7.0 %collective-permute-start.14 = (bf16[1024,512]{1,0:T(8,128)(2,1)}, bf16[1024,512]{1,0:T(8,128)(2,1)S(1)}, u32[]{:S(2)}, u32[]{:S(2)}) collective-permute-start(bf16[1024,512]{1,0:T(8,128)(2,1)} %constant_dynamic-slice_fusion), channel_id=1, source_target_pairs={{0,0},{1,32},{2,64},{3,96},{4,4},{5,36},{6,68},{7,100},{8,8},{9,40... | collective-permute-start | bytes 3145736 | tf_op jit(solution)/shard_map/ppermute | solution.py:37
  126.1 5.8 %collective-permute-start.13 = (bf16[64,1024]{1,0:T(8,128)(2,1)S(1)}, bf16[64,1024]{1,0:T(8,128)(2,1)S(1)}, u32[]{:S(2)}, u32[]{:S(2)}) collective-permute-start(bf16[64,1024]{1,0:T(8,128)(2,1)S(1)} %slice.166), channel_id=1, source_target_pairs={{0,4},{1,5},{2,6},{3,7},{8,12},{9,13},{10,14},{11,15},{16,20},{17,... | collective-permute-start | bytes 393224 | tf_op jit(solution)/shard_map/ppermute | solution.py:37
  135.6 5.6 %collective-permute-done.14.up_ref = bf16[1024,512]{1,0:T(8,128)(2,1)S(1)} collective-permute-done((bf16[1024,512]{1,0:T(8,128)(2,1)}, bf16[1024,512]{1,0:T(8,128)(2,1)S(1)}, u32[]{:S(2)}, u32[]{:S(2)}) %collective-permute-start.14) | collective-permute-done | bytes 1048608 | tf_op jit(solution)/shard_map/ppermute | solution.py:37
  143.0 7.2 %all-to-all-start.1 = ((bf16[16,64,1152]{2,1,0:T(8,128)(2,1)}), bf16[16,64,1152]{2,1,0:T(8,128)(2,1)S(1)}, u32[]{:S(2)}, u32[]{:S(2)}) async-start(bf16[16,64,1152]{2,1,0:T(8,128)(2,1)} %broadcast_in_dim.114), calls=%async_computation.1 | async-start | bytes 4718592 | tf_op jit(solution)/shard_map/all_to_all | solution.py:57
  154.3 28.5 %all-to-all-done.1 = bf16[16,64,1152]{2,1,0:T(8,128)(2,1)S(1)} async-done(((bf16[16,64,1152]{2,1,0:T(8,128)(2,1)}), bf16[16,64,1152]{2,1,0:T(8,128)(2,1)S(1)}, u32[]{:S(2)}, u32[]{:S(2)}) %all-to-all-start.1) | async-done | bytes 2359328 | tf_op jit(solution)/shard_map/all_to_all | solution.py:57
  195.9 5.4 %all-to-all-start.2 = ((bf16[4,128,512]{2,1,0:T(8,128)(2,1)}), bf16[4,128,512]{2,1,0:T(8,128)(2,1)S(1)}, u32[]{:S(2)}, u32[]{:S(2)}) async-start(bf16[4,128,512]{2,1,0:T(8,128)(2,1)} %bitcast.31), calls=%async_computation.2 | async-start | bytes 1048576 | tf_op jit(solution)/shard_map/all_to_all | solution.py:57
  201.2 8.9 %all-to-all-done.2 = bf16[4,128,512]{2,1,0:T(8,128)(2,1)S(1)} async-done(((bf16[4,128,512]{2,1,0:T(8,128)(2,1)}), bf16[4,128,512]{2,1,0:T(8,128)(2,1)S(1)}, u32[]{:S(2)}, u32[]{:S(2)}) %all-to-all-start.2) | async-done | bytes 524320 | tf_op jit(solution)/shard_map/all_to_all | solution.py:57
  210.3 10.4 %all_to_all.35 = bf16[4,128,512]{2,1,0:T(8,128)(2,1)S(1)} all-to-all(bf16[4,128,512]{2,1,0:T(8,128)(2,1)S(1)} %broadcast_in_dim.118), channel_id=1, replica_groups=mesh['z'=4,'y'=4,'pipe'=2,'xl'=2,'core'=2] {'pipe','xl'}, dimensions={0} | all-to-all | bytes 1048576 | tf_op jit(solution)/shard_map/all_to_all | solution.py:57
  227.1 39.0 %all_to_all.36 = bf16[16,64,1408]{2,1,0:T(8,128)(2,1)S(1)} all-to-all(bf16[16,64,1408]{2,1,0:T(8,128)(2,1)S(1)} %bitcast.182), channel_id=1, replica_groups=mesh['z'=4,'y'=4,'pipe'=2,'xl'=2,'core'=2] {'z','y'}, dimensions={0} | all-to-all | bytes 5767168 | tf_op jit(solution)/shard_map/all_to_all | solution.py:57
  287.6 31.9 %all_to_all.37 = bf16[16,64,1152]{2,1,0:T(8,128)(2,1)S(1)} all-to-all(bf16[16,64,1152]{2,1,0:T(8,128)(2,1)S(1)} %broadcast_in_dim.119), channel_id=1, replica_groups=mesh['z'=4,'y'=4,'pipe'=2,'xl'=2,'core'=2] {'z','y'}, dimensions={0} | all-to-all | bytes 4718592 | tf_op jit(solution)/shard_map/all_to_all | solution.py:57
  322.5 4.1 %collective-permute-start.19 = (bf16[16,32,512]{2,1,0:T(8,128)(2,1)S(1)}, bf16[16,32,512]{2,1,0:T(8,128)(2,1)S(1)}, u32[]{:S(2)}, u32[]{:S(2)}) collective-permute-start(bf16[16,32,512]{2,1,0:T(8,128)(2,1)S(1)} %dynamic-slice_bitcast_fusion.3), channel_id=1, source_target_pairs={{0,1},{1,0},{2,3},{3,2},{4,5},{5,4},{6,7},{7,6},{8,9},{9,8},{10,11... | collective-permute-start | bytes 1572872 | tf_op jit(solution)/shard_map/ppermute | solution.py:37
  329.1 3.9 %all-to-all-start.6 = ((bf16[4,128,512]{2,1,0:T(8,128)(2,1)}), bf16[4,128,512]{2,1,0:T(8,128)(2,1)S(1)}, u32[]{:S(2)}, u32[]{:S(2)}) async-start(bf16[4,128,512]{2,1,0:T(8,128)(2,1)} %bitcast.45), calls=%async_computation.6 | async-start | bytes 1048576 | tf_op jit(solution)/shard_map/all_to_all | solution.py:57
  333.0 8.9 %all-to-all-done.6 = bf16[4,128,512]{2,1,0:T(8,128)(2,1)S(1)} async-done(((bf16[4,128,512]{2,1,0:T(8,128)(2,1)}), bf16[4,128,512]{2,1,0:T(8,128)(2,1)S(1)}, u32[]{:S(2)}, u32[]{:S(2)}) %all-to-all-start.6) | async-done | bytes 524320 | tf_op jit(solution)/shard_map/all_to_all | solution.py:57
  345.6 4.0 %collective-permute-start.23 = (bf16[32,512]{1,0:T(8,128)(2,1)S(1)}, bf16[32,512]{1,0:T(8,128)(2,1)S(1)}, u32[]{:S(2)}, u32[]{:S(2)}) collective-permute-start(bf16[32,512]{1,0:T(8,128)(2,1)S(1)} %get-tuple-element.67), channel_id=1, source_target_pairs={{0,8},{1,12},{2,40},{3,44},{4,72},{5,76},{6,104},{7,108},{8,16},{9... | collective-permute-start | bytes 98312 | tf_op jit(solution)/shard_map/ppermute | solution.py:37
  (229 shorter events, 128.0 us)
Async XLA Ops:
  2.4 16.7 %collective-permute-start.3 = (bf16[80,512]{1,0:T(8,128)(2,1)}, bf16[80,512]{1,0:T(8,128)(2,1)S(1)}, u32[]{:S(2)}, u32[]{:S(2)}) collective-permute-start(bf16[80,512]{1,0:T(8,128)(2,1)} %get-tuple-element.83), channel_id=1, source_target_pairs={{0,8},{1,40},{2,72},{3,104},{4,12},{5,44},{6,76},{7,108},{8,16},{9... | collective-permute-start | bytes 245768 | tf_op jit(solution)/shard_map/ppermute | solution.py:37
  6.4 12.7 %collective-permute-start = (bf16[80,512]{1,0:T(8,128)(2,1)}, bf16[80,512]{1,0:T(8,128)(2,1)S(1)}, u32[]{:S(2)}, u32[]{:S(2)}) collective-permute-start(bf16[80,512]{1,0:T(8,128)(2,1)} %get-tuple-element.84), channel_id=1, source_target_pairs={{0,0},{1,32},{2,64},{3,96},{4,4},{5,36},{6,68},{7,100},{8,8},{9,40... | collective-permute-start | bytes 245768 | tf_op jit(solution)/shard_map/ppermute | solution.py:37
  8.3 10.7 %collective-permute-start.1 = (bf16[80,512]{1,0:T(8,128)(2,1)}, bf16[80,512]{1,0:T(8,128)(2,1)S(1)}, u32[]{:S(2)}, u32[]{:S(2)}) collective-permute-start(bf16[80,512]{1,0:T(8,128)(2,1)} %get-tuple-element.85), channel_id=1, source_target_pairs={{0,24},{1,56},{2,88},{3,120},{4,28},{5,60},{6,92},{7,124},{8,0},{9... | collective-permute-start | bytes 245768 | tf_op jit(solution)/shard_map/ppermute | solution.py:37
  11.2 7.8 %collective-permute-start.2 = (bf16[80,512]{1,0:T(8,128)(2,1)S(1)}, bf16[80,512]{1,0:T(8,128)(2,1)}, u32[]{:S(2)}, u32[]{:S(2)}) collective-permute-start(bf16[80,512]{1,0:T(8,128)(2,1)S(1)} %get-tuple-element.86), channel_id=1, source_target_pairs={{0,16},{1,48},{2,80},{3,112},{4,20},{5,52},{6,84},{7,116},{8,24},{... | collective-permute-start | bytes 245768 | tf_op jit(solution)/shard_map/ppermute | solution.py:37
  16.3 12.3 %collective-permute-start.4 = (bf16[176,1280]{1,0:T(8,128)(2,1)}, bf16[176,1280]{1,0:T(8,128)(2,1)}, u32[]{:S(2)}, u32[]{:S(2)}) collective-permute-start(bf16[176,1280]{1,0:T(8,128)(2,1)} %slice.149), channel_id=1, source_target_pairs={{0,4},{1,5},{2,6},{3,7},{4,0},{5,1},{6,2},{7,3},{8,12},{9,13},{10,... | collective-permute-start | bytes 1351688 | tf_op jit(solution)/shard_map/ppermute | solution.py:37
  29.4 13.4 %collective-permute-start.6 = (bf16[176,1280]{1,0:T(8,128)(2,1)}, bf16[176,1280]{1,0:T(8,128)(2,1)}, u32[]{:S(2)}, u32[]{:S(2)}) collective-permute-start(bf16[176,1280]{1,0:T(8,128)(2,1)} %slice.114), channel_id=1, source_target_pairs={{0,4},{1,5},{2,6},{3,7},{4,0},{5,1},{6,2},{7,3},{8,12},{9,13},{10,... | collective-permute-start | bytes 1351688 | tf_op jit(solution)/shard_map/ppermute | solution.py:37
  32.9 20.0 %collective-permute-start.5 = (bf16[4,80,512]{2,1,0:T(8,128)(2,1)}, bf16[4,80,512]{2,1,0:T(8,128)(2,1)}, u32[]{:S(2)}, u32[]{:S(2)}) collective-permute-start(bf16[4,80,512]{2,1,0:T(8,128)(2,1)} %constant_dynamic-slice_fusion.1), channel_id=1, source_target_pairs={{0,2},{1,3},{2,0},{3,1},{4,6},{5,7},{6,4},{7,5},{8,10},{9,11},{10,... | collective-permute-start | bytes 983048 | tf_op jit(solution)/shard_map/ppermute | solution.py:37
  42.9 17.8 %collective-permute-start.8 = (bf16[160,1280]{1,0:T(8,128)(2,1)S(1)}, bf16[160,1280]{1,0:T(8,128)(2,1)S(1)}, u32[]{:S(2)}, u32[]{:S(2)}) collective-permute-start(bf16[160,1280]{1,0:T(8,128)(2,1)S(1)} %slice.120), channel_id=1, source_target_pairs={{0,4},{1,5},{2,6},{3,7},{4,0},{5,1},{6,2},{7,3},{8,12},{9,13},{10,... | collective-permute-start | bytes 1228808 | tf_op jit(solution)/shard_map/ppermute | solution.py:37
  54.0 8.3 %collective-permute-start.7 = (bf16[2,4,80,512]{3,2,1,0:T(8,128)(2,1)S(1)}, bf16[2,4,80,512]{3,2,1,0:T(8,128)(2,1)S(1)}, u32[]{:S(2)}, u32[]{:S(2)}) collective-permute-start(bf16[2,4,80,512]{3,2,1,0:T(8,128)(2,1)S(1)} %pad_maximum_fusion.2), channel_id=1, source_target_pairs={{0,1},{1,0},{2,3},{3,2},{4,5},{5,4},{6,7},{7,6},{8,9},{9,8},{10,11... | collective-permute-start | bytes 1966088 | tf_op jit(solution)/shard_map/ppermute | solution.py:37
  66.9 40.2 %all-to-all-start = ((bf16[16,64,1280]{2,1,0:T(8,128)(2,1)}), bf16[16,64,1280]{2,1,0:T(8,128)(2,1)}, u32[]{:S(2)}, u32[]{:S(2)}) async-start(bf16[16,64,1280]{2,1,0:T(8,128)(2,1)} %bitcast.15), calls=%async_computation | async-start | bytes 5242880 | tf_op jit(solution)/shard_map/all_to_all | solution.py:57
  74.5 28.2 %collective-permute-start.10 = (f32[1,64]{1,0:T(1,128)S(1)}, f32[1,64]{1,0:T(1,128)S(1)}, u32[]{:S(2)}, u32[]{:S(2)}) collective-permute-start(f32[1,64]{1,0:T(1,128)S(1)} %bitcast.209), channel_id=1, source_target_pairs={{0,2},{1,3},{2,0},{3,1},{4,6},{5,7},{6,4},{7,5},{8,10},{9,11},{10,... | collective-permute-start | bytes 776 | tf_op jit(solution)/shard_map/ppermute | solution.py:37
  75.9 29.9 %collective-permute-start.9 = (bf16[1024,512]{1,0:T(8,128)(2,1)}, bf16[1024,512]{1,0:T(8,128)(2,1)S(1)}, u32[]{:S(2)}, u32[]{:S(2)}) collective-permute-start(bf16[1024,512]{1,0:T(8,128)(2,1)} %dynamic-slice_bitcast_fusion), channel_id=1, source_target_pairs={{0,4},{1,5},{2,6},{3,7},{4,0},{5,1},{6,2},{7,3},{8,12},{9,13},{10,... | collective-permute-start | bytes 3145736 | tf_op jit(solution)/shard_map/ppermute | solution.py:37
  102.8 7.7 %collective-permute-start.11 = (f32[1,64]{1,0:T(1,128)S(1)}, f32[1,64]{1,0:T(1,128)S(1)}, u32[]{:S(2)}, u32[]{:S(2)}) collective-permute-start(f32[1,64]{1,0:T(1,128)S(1)} %bitcast_add_fusion.1), channel_id=1, source_target_pairs={{0,1},{1,0},{2,3},{3,2},{4,5},{5,4},{6,7},{7,6},{8,9},{9,8},{10,11... | collective-permute-start | bytes 776 | tf_op jit(solution)/shard_map/ppermute | solution.py:37
  109.2 8.3 %collective-permute-start.12 = (bf16[64,1280]{1,0:T(8,128)(2,1)S(1)}, bf16[64,1280]{1,0:T(8,128)(2,1)S(1)}, u32[]{:S(2)}, u32[]{:S(2)}) collective-permute-start(bf16[64,1280]{1,0:T(8,128)(2,1)S(1)} %reduce_sum.97), channel_id=1, source_target_pairs={{4,0},{5,1},{6,2},{7,3},{12,8},{13,9},{14,10},{15,11},{20,16},{21,... | collective-permute-start | bytes 491528 | tf_op jit(solution)/shard_map/ppermute | solution.py:37
  110.5 30.7 %collective-permute-start.14 = (bf16[1024,512]{1,0:T(8,128)(2,1)}, bf16[1024,512]{1,0:T(8,128)(2,1)S(1)}, u32[]{:S(2)}, u32[]{:S(2)}) collective-permute-start(bf16[1024,512]{1,0:T(8,128)(2,1)} %constant_dynamic-slice_fusion), channel_id=1, source_target_pairs={{0,0},{1,32},{2,64},{3,96},{4,4},{5,36},{6,68},{7,100},{8,8},{9,40... | collective-permute-start | bytes 3145736 | tf_op jit(solution)/shard_map/ppermute | solution.py:37
  126.1 9.5 %collective-permute-start.13 = (bf16[64,1024]{1,0:T(8,128)(2,1)S(1)}, bf16[64,1024]{1,0:T(8,128)(2,1)S(1)}, u32[]{:S(2)}, u32[]{:S(2)}) collective-permute-start(bf16[64,1024]{1,0:T(8,128)(2,1)S(1)} %slice.166), channel_id=1, source_target_pairs={{0,4},{1,5},{2,6},{3,7},{8,12},{9,13},{10,14},{11,15},{16,20},{17,... | collective-permute-start | bytes 393224 | tf_op jit(solution)/shard_map/ppermute | solution.py:37
  143.0 39.8 %all-to-all-start.1 = ((bf16[16,64,1152]{2,1,0:T(8,128)(2,1)}), bf16[16,64,1152]{2,1,0:T(8,128)(2,1)S(1)}, u32[]{:S(2)}, u32[]{:S(2)}) async-start(bf16[16,64,1152]{2,1,0:T(8,128)(2,1)} %broadcast_in_dim.114), calls=%async_computation.1 | async-start | bytes 4718592 | tf_op jit(solution)/shard_map/all_to_all | solution.py:57
  195.9 14.3 %all-to-all-start.2 = ((bf16[4,128,512]{2,1,0:T(8,128)(2,1)}), bf16[4,128,512]{2,1,0:T(8,128)(2,1)S(1)}, u32[]{:S(2)}, u32[]{:S(2)}) async-start(bf16[4,128,512]{2,1,0:T(8,128)(2,1)} %bitcast.31), calls=%async_computation.2 | async-start | bytes 1048576 | tf_op jit(solution)/shard_map/all_to_all | solution.py:57
  280.0 7.2 %collective-permute-start.18 = (bf16[64,1024]{1,0:T(8,128)(2,1)S(1)}, bf16[64,1024]{1,0:T(8,128)(2,1)S(1)}, u32[]{:S(2)}, u32[]{:S(2)}) collective-permute-start(bf16[64,1024]{1,0:T(8,128)(2,1)S(1)} %slice.181), channel_id=1, source_target_pairs={{4,0},{5,1},{6,2},{7,3},{12,8},{13,9},{14,10},{15,11},{20,16},{21,... | collective-permute-start | bytes 393224 | tf_op jit(solution)/shard_map/ppermute | solution.py:37
  322.5 5.6 %collective-permute-start.19 = (bf16[16,32,512]{2,1,0:T(8,128)(2,1)S(1)}, bf16[16,32,512]{2,1,0:T(8,128)(2,1)S(1)}, u32[]{:S(2)}, u32[]{:S(2)}) collective-permute-start(bf16[16,32,512]{2,1,0:T(8,128)(2,1)S(1)} %dynamic-slice_bitcast_fusion.3), channel_id=1, source_target_pairs={{0,1},{1,0},{2,3},{3,2},{4,5},{5,4},{6,7},{7,6},{8,9},{9,8},{10,11... | collective-permute-start | bytes 1572872 | tf_op jit(solution)/shard_map/ppermute | solution.py:37
  329.1 12.8 %all-to-all-start.6 = ((bf16[4,128,512]{2,1,0:T(8,128)(2,1)}), bf16[4,128,512]{2,1,0:T(8,128)(2,1)S(1)}, u32[]{:S(2)}, u32[]{:S(2)}) async-start(bf16[4,128,512]{2,1,0:T(8,128)(2,1)} %bitcast.45), calls=%async_computation.6 | async-start | bytes 1048576 | tf_op jit(solution)/shard_map/all_to_all | solution.py:57
  342.0 13.6 %collective-permute-start.20 = (bf16[32,512]{1,0:T(8,128)(2,1)S(1)}, bf16[32,512]{1,0:T(8,128)(2,1)S(1)}, u32[]{:S(2)}, u32[]{:S(2)}) collective-permute-start(bf16[32,512]{1,0:T(8,128)(2,1)S(1)} %get-tuple-element.70), channel_id=1, source_target_pairs={{0,0},{1,4},{2,32},{3,36},{4,64},{5,68},{6,96},{7,100},{8,8},{9,12... | collective-permute-start | bytes 98312 | tf_op jit(solution)/shard_map/ppermute | solution.py:37
  345.6 11.4 %collective-permute-start.23 = (bf16[32,512]{1,0:T(8,128)(2,1)S(1)}, bf16[32,512]{1,0:T(8,128)(2,1)S(1)}, u32[]{:S(2)}, u32[]{:S(2)}) collective-permute-start(bf16[32,512]{1,0:T(8,128)(2,1)S(1)} %get-tuple-element.67), channel_id=1, source_target_pairs={{0,8},{1,12},{2,40},{3,44},{4,72},{5,76},{6,104},{7,108},{8,16},{9... | collective-permute-start | bytes 98312 | tf_op jit(solution)/shard_map/ppermute | solution.py:37
  349.6 7.4 %collective-permute-start.22 = (bf16[32,512]{1,0:T(8,128)(2,1)S(1)}, bf16[32,512]{1,0:T(8,128)(2,1)S(1)}, u32[]{:S(2)}, u32[]{:S(2)}) collective-permute-start(bf16[32,512]{1,0:T(8,128)(2,1)S(1)} %get-tuple-element.68), channel_id=1, source_target_pairs={{0,16},{1,20},{2,48},{3,52},{4,80},{5,84},{6,112},{7,116},{8,24},{... | collective-permute-start | bytes 98312 | tf_op jit(solution)/shard_map/ppermute | solution.py:37
  (25 other events, 218.8 us)
where the time goes:
time: 360 us; the launch traced here: 358 us
  starting transfers between devices  101 us (28%)
  waiting for transfers between devices  81.7 us (23%)
  blocking collectives  81.3 us (23%)
  local copies, waits for them, and re-layouts  43.8 us (12%)
  matrix products  19.8 us (6%)
  other arithmetic  18.6 us (5%)
  Pallas kernels  11 us (3%)
    all_to_all x3, blocking collectives, exchange(): return lax.all_to_all(blocks, axes, 0, 0, tiled=True)  81.3 us
    ppermute x24, starting transfers between devices, send(): return lax.ppermute(block, AXES, pairs)  76.6 us
    all_to_all x4, waiting for transfers between devices, exchange(): return lax.all_to_all(blocks, axes, 0, 0, tiled=True)  47.5 us
    ppermute x24, waiting for transfers between devices, send(): return lax.ppermute(block, AXES, pairs)  34.2 us
    all_to_all x4, starting transfers between devices, exchange(): return lax.all_to_all(blocks, axes, 0, 0, tiled=True)  23.9 us
    unnamed x64, local copies, waits for them, and re-layouts  14 us
  transfers between devices with their start and end apart: 28, of which 14 were waited for; matrix products, arithmetic and copies ran while one was open for 16% of the time, Pallas kernels for 0%

commit v1 on v0

v1 whole, which is shorter than its diff:
```python
import jax
import jax.numpy as jnp
from jax import lax
from jax.experimental import pallas as pl
from jax.experimental.pallas import tpu as pltpu
from jax.sharding import Mesh
from jax.sharding import PartitionSpec as P

HEAD = 128
RANK = 128
ADAPTERS = 8
CTX = 80
EPS = 1e-05
SCALE = 64.0
LANES = 128
PIECES = 1
AXES = ("z", "y", "pipe", "xl", "core")
DP = ("z", "y")
RING = ("pipe", "xl")
bf16 = jnp.bfloat16
f32 = jnp.float32


def send(block, route):
    pairs = []
    for z in range(4):
        for y in range(4):
            for p in range(2):
                for xl in range(2):
                    for c in range(2):
                        there = route(z, y, p, xl, c)
                        if there is None:
                            continue
                        source = ((z * 4 + y) * 2 + p) * 4 + xl * 2 + c
                        a, b, q, u, v = there
                        target = (((a % 4) * 4 + b % 4) * 2 + q) * 4 + u * 2 + v
                        pairs.append((source, target))
    return lax.ppermute(block, AXES, pairs)


def ring(step):
    def route(z, y, p, u, c):
        there = (2 * p + u + step) % 4
        return (z, y, there // 2, there % 2, c)

    return route


def other_core(z, y, p, u, c):
    return (z, y, p, u, 1 - c)


def other_xl(z, y, p, u, c):
    return (z, y, p, 1 - u, c)


def other_pipe(z, y, p, u, c):
    return (z, y, 1 - p, 1 - u, c)


def pipe_from(source):
    return lambda z, y, p, u, c: other_pipe(z, y, p, u, c) if p == source else None


def exchange(blocks, axes):
    return lax.all_to_all(blocks, axes, 0, 0, tiled=True)


def after(value, earlier):
    return lax.optimization_barrier((value, earlier))[0]


def project_in_kernel(rows, x_ref, w_ref, out_ref):
    x = x_ref[...]
    heads = w_ref.shape[1] // LANES
    result = jnp.dot(x, w_ref[...], preferred_element_type=f32).astype(bf16)
    ones = jnp.ones((16, x.shape[1]), f32)
    first = lax.broadcasted_iota(jnp.int32, (16, LANES), 0) == 0
    for i in range(out_ref.shape[0]):
        mine = slice(i * rows, (i + 1) * rows)
        for j in range(heads):
            out_ref[i, j * rows : (j + 1) * rows] = result[mine, j * LANES : (j + 1) * LANES]
        squares = x[mine].astype(f32)
        rest = jnp.zeros((LANES - rows, x.shape[1]), f32)
        squares = jnp.concatenate([squares * squares, rest], axis=0)
        total = lax.dot_general(ones, squares, (((1,), (1,)), ((), ())), preferred_element_type=f32)
        high = total.astype(bf16).astype(f32)
        out_ref[i, heads * rows :] = jnp.where(first, high, total - high).astype(bf16)


def project_in(state, weights, rows, groups=4):
    count, depth = state.shape
    width = weights.shape[1]
    length = width // LANES * rows + 16
    return pl.pallas_call(
        lambda *refs: project_in_kernel(rows, *refs),
        grid=(count // (rows * groups),),
        in_specs=[
            pl.BlockSpec((rows * groups, depth), lambda i: (i, 0)),
            pl.BlockSpec((depth, width), lambda i: (0, 0)),
        ],
        out_specs=pl.BlockSpec((groups, length, LANES), lambda i: (i, 0, 0)),
        out_shape=jax.ShapeDtypeStruct((count // rows, length, LANES), bf16),
        compiler_params=pltpu.CompilerParams(vmem_limit_bytes=32 * 1024 * 1024),
        cost_estimate=pl.CostEstimate(flops=0, bytes_accessed=0, transcendentals=0),
    )(state, weights)


def project_out_kernel(rows, _, a_ref, ids_ref, w_ref, up_ref, out_ref):
    heads = w_ref.shape[0] // LANES
    lhs, shrunk = [], []
    for i in range(a_ref.shape[0]):
        pieces = [a_ref[i, j * rows : (j + 1) * rows] for j in range(heads + 1)]
        lhs.append(jnp.concatenate(pieces[:heads], axis=1))
        shrunk.append(pieces[heads])
    lhs, shrunk = jnp.concatenate(lhs, axis=0), jnp.concatenate(shrunk, axis=0)
    total = jnp.dot(lhs, w_ref[...], preferred_element_type=f32)
    ids = ids_ref[...]
    nothing = jnp.zeros_like(shrunk)
    spread = jnp.concatenate(
        [jnp.where(ids == a, shrunk, nothing) for a in range(ADAPTERS)], axis=1
    )
    total = total + jnp.dot(spread, up_ref[...], preferred_element_type=f32)
    out_ref[...] = total.astype(bf16)


def project_out(load, ids, weights, up, rows, first, steps=2, groups=4):
    count, length, _ = load.shape
    depth, width = weights.shape
    tile = groups * rows
    return pl.pallas_call(
        lambda *refs: project_out_kernel(rows, *refs),
        grid_spec=pltpu.PrefetchScalarGridSpec(
            num_scalar_prefetch=1,
            grid=(steps,),
            in_specs=[
                pl.BlockSpec((groups, length, LANES), lambda i, f: (f[0] + i, 0, 0)),
                pl.BlockSpec((tile, RANK), lambda i, f: (f[0] + i, 0)),
                pl.BlockSpec((depth, width), lambda i, f: (0, 0)),
                pl.BlockSpec((ADAPTERS * RANK, width), lambda i, f: (0, 0)),
            ],
            out_specs=pl.BlockSpec((tile, width), lambda i, f: (i, 0)),
        ),
        out_shape=jax.ShapeDtypeStruct((steps * tile, width), bf16),
        compiler_params=pltpu.CompilerParams(vmem_limit_bytes=32 * 1024 * 1024),
        cost_estimate=pl.CostEstimate(flops=10**9, bytes_accessed=5 * 10**6, transcendentals=0),
    )(first.astype(jnp.int32).reshape(1), load, ids, weights, up)


def rope_tables(positions):
    half = HEAD // 2
    inv_freq = jnp.exp(-jnp.log(10000.0) * jnp.arange(half, dtype=f32) * (2.0 / HEAD))
    angles = positions.astype(f32)[:, None] * inv_freq[None, :]
    return (jnp.cos(angles), jnp.sin(angles))


def attention_kernel(
    g, x_ref, factor_ref, cos_ref, sin_ref, bias_ref, k_ref, v_ref, out_ref
):
    cos, sin = cos_ref[...], sin_ref[...]
    inverse = float(HEAD) ** -0.5
    x = x_ref[...].astype(f32) * factor_ref[...]
    heads = x.shape[1] // LANES - 2

    def turn(piece):
        return (piece * cos + pltpu.roll(piece, HEAD // 2, 1) * sin).astype(bf16)

    query = [turn(x[:, j * LANES : (j + 1) * LANES]) for j in range(heads)]
    key_new = turn(x[:, heads * LANES : (heads + 1) * LANES]).astype(f32)
    value_new = x[:, (heads + 1) * LANES :].astype(bf16).astype(f32)
    query = jnp.stack([q.astype(f32) for q in query], axis=1)
    keys = k_ref[:, :, g * HEAD : (g + 1) * HEAD]
    values = v_ref[:, :, g * HEAD : (g + 1) * HEAD]
    scores = jnp.einsum("rhd,rcd->rhc", query.astype(bf16), keys, preferred_element_type=f32)
    scores = scores * inverse + bias_ref[...]
    own = jnp.sum(query * key_new[:, None, :], axis=-1, keepdims=True) * inverse
    top = jnp.maximum(jnp.max(scores, axis=-1, keepdims=True), own)
    raw = jnp.exp(scores - top)
    own_raw = jnp.exp(own - top)
    total = jnp.sum(raw, axis=-1, keepdims=True) + own_raw
    weights = (raw / total).astype(bf16)
    own_weight = (own_raw / total).astype(bf16).astype(f32)
    out = jnp.einsum("rhc,rcd->rhd", weights, values, preferred_element_type=f32)
    out = out + own_weight * value_new[:, None, :]
    for j in range(heads):
        out_ref[j] = out[:, j, :].astype(bf16)


def attention(g, x, *rest):
    rows = x.shape[0]
    heads = x.shape[1] // LANES - 2
    return pl.pallas_call(
        lambda *refs: attention_kernel(g, *refs),
        in_specs=[pl.BlockSpec(memory_space=pltpu.VMEM)] * 7,
        out_specs=pl.BlockSpec(memory_space=pltpu.VMEM),
        out_shape=jax.ShapeDtypeStruct((heads, rows, HEAD), bf16),
        compiler_params=pltpu.CompilerParams(vmem_limit_bytes=40 * 1024 * 1024),
        cost_estimate=pl.CostEstimate(flops=10**9, bytes_accessed=5 * 10**6, transcendentals=0),
    )(x, *rest)


def shrink_kernel(low_ref, high_ref, down_ref, ids_ref, gate_ref, out_ref):
    flat = [ref[j] for ref in (low_ref, high_ref) for j in range(ref.shape[0])]
    product = jnp.dot(jnp.concatenate(flat, axis=1), down_ref[...], preferred_element_type=f32)
    ids = ids_ref[...]
    total = jnp.zeros(ids.shape, f32)
    for a in range(ADAPTERS):
        total = total + jnp.where(ids == a, product[:, a * RANK : (a + 1) * RANK], 0.0)
    out_ref[...] = (total * gate_ref[...]).astype(bf16)


def shrink(low, high, down, ids, gate):
    return pl.pallas_call(
        shrink_kernel,
        in_specs=[pl.BlockSpec(memory_space=pltpu.VMEM)] * 5,
        out_specs=pl.BlockSpec(memory_space=pltpu.VMEM),
        out_shape=jax.ShapeDtypeStruct(ids.shape, bf16),
        compiler_params=pltpu.CompilerParams(vmem_limit_bytes=40 * 1024 * 1024),
        cost_estimate=pl.CostEstimate(flops=10**9, bytes_accessed=5 * 10**6, transcendentals=0),
    )(low, high, down, ids, gate)


def on_device(
    residual_input,
    layer_norm_gain,
    query_weight,
    key_weight,
    value_weight,
    output_weight,
    adapter_down_weight,
    adapter_up_weight,
    cached_key_rows,
    cached_value_rows,
    request_adapter,
    rank_per_adapter,
    cached_length,
):
    z, y, p = lax.axis_index("z"), lax.axis_index("y"), lax.axis_index("pipe")
    xl, core = lax.axis_index("xl"), lax.axis_index("core")
    x = 2 * p + xl
    group = residual_input.shape[0]
    half = group // 2
    block = query_weight.shape[1]
    qh = query_weight.shape[2] // 2
    kh = key_weight.shape[2] // 2

    gain = lax.dynamic_slice_in_dim(layer_norm_gain[0], (4 * z + y) * block, block, 0)
    gain = gain.astype(f32)[:, None]

    def in_half(which):
        parts = [
            lax.dynamic_slice_in_dim(query_weight[0], which * qh, qh, 1),
            lax.dynamic_slice_in_dim(key_weight[0], which * kh, kh, 1),
            lax.dynamic_slice_in_dim(value_weight[0], which * kh, kh, 1),
        ]
        return (jnp.concatenate(parts, axis=1).astype(f32) * gain).astype(bf16)

    numbers = jnp.pad(request_adapter.astype(bf16).reshape(1, group), ((0, 15), (0, block - group)))
    turned = jnp.concatenate([residual_input, jnp.concatenate([numbers] * 4, axis=1)], axis=0)
    turned = send(turned, lambda z, y, p, u, c: (2 * u + c, y, p, z // 2, z % 2))
    theirs_in = in_half(1 - p)
    cut = block // 32 * 29
    in_first = send(theirs_in[:cut], other_pipe)
    in_rest = send(after(theirs_in, in_first)[cut:], other_pipe)
    turned = jnp.stack([turned[:, k * block : (k + 1) * block] for k in range(4)])
    quarter = exchange(turned, "y")
    near = send(quarter, other_xl)
    down = adapter_down_weight[0].reshape(-1, ADAPTERS * RANK)
    out_mine = lax.dynamic_slice_in_dim(output_weight[0], p * qh, qh, 0)
    out_theirs = lax.dynamic_slice_in_dim(output_weight[0], (1 - p) * qh, qh, 0)
    up = adapter_up_weight[0].reshape(ADAPTERS * RANK, -1)
    up = lax.dynamic_slice_in_dim(up, y * block, block, 1)
    near, down, out_theirs, up = lax.optimization_barrier((near, down, out_theirs, up))
    pair = jnp.stack([jnp.where(xl == 0, quarter, near), jnp.where(xl == 0, near, quarter)])
    far = send(pair, other_core)
    even, odd = jnp.where(core == 0, pair, far), jnp.where(core == 0, far, pair)
    rows = jnp.stack([even[0], odd[0], even[1], odd[1]])
    in_got = jnp.concatenate([in_first, in_rest], axis=0)
    size = group // PIECES
    spans = [slice(i * size, (i + 1) * size) for i in range(PIECES)]
    state = [rows[:, :, span].reshape(-1, block) for span in spans]
    ids = [rows[:, :, group, span].reshape(-1, 1) for span in spans]
    ids = [jnp.broadcast_to(part, (part.shape[0], RANK)) for part in ids]

    square = residual_input.astype(f32)
    square = jnp.sum(square * square, axis=1).reshape(1, group)
    square = square + send(square, other_xl)
    square = square + send(square, other_core)
    square = square.reshape(group, 1)

    chosen = request_adapter[:, None] == jnp.arange(ADAPTERS, dtype=jnp.int32)[None, :]
    rank = jnp.sum(jnp.where(chosen, rank_per_adapter[None, :], 0), axis=1)
    live = jnp.arange(RANK, dtype=jnp.int32)[None, :] < rank[:, None]
    rank_scale = SCALE / rank.astype(f32)
    gate = jnp.where(live, rank_scale[:, None], 0.0)
    own_ids = jnp.broadcast_to(request_adapter[:, None], (group, RANK))
    cosine, sine = rope_tables(cached_length)
    cosine = jnp.concatenate([cosine, cosine], axis=1)
    sine = jnp.concatenate([-sine, sine], axis=1)
    bias = jnp.arange(CTX, dtype=jnp.int32)[None, None, :] < cached_length[:, None, None]
    bias = jnp.where(bias, 0.0, -1e30).astype(f32)
    features = 4.0 * residual_input.shape[1]

    def later_weights(earlier):
        mine, theirs, own = after((out_mine, out_theirs, up), earlier)
        theirs = send(theirs, other_pipe)
        near = send(own, lambda z, y, p, u, c: (z, y, p, 1 - u, c) if 2 * u + c == z else None)
        own = jnp.where(2 * xl + core == z, own, near)
        far = send(own, lambda z, y, p, u, c: (z, y, p, u, 1 - c) if c == z % 2 else None)
        own = jnp.where(core == z % 2, own, far)
        return jnp.where(p == 0, mine, theirs), jnp.where(p == 1, mine, theirs), own

    def summed(layer, i, weights, previous):
        if layer == 1:
            parts = project_in(state[i], weights, size)
        else:
            parts = jnp.dot(state[i], weights, preferred_element_type=f32).astype(bf16)
            parts = parts.reshape(16, size, -1)
        parts = parts if previous is None else after(parts, previous)
        if layer == 0 and i == 0:
            w_out.extend(later_weights(parts))
        parts = exchange(parts, DP)
        if layer == 0 and i == 0:
            parts, *w_out[:] = lax.optimization_barrier((parts, *w_out))
        sums = jnp.sum(parts.astype(f32), axis=0)
        if layer == 0:
            return parts, sums.astype(bf16), square[spans[i]]
        ours = sums[:-16].reshape(-1, size, LANES).transpose(1, 0, 2).reshape(size, -1)
        squares = (sums[-16, :size] + sums[-15, :size]).reshape(size, 1)
        return parts, ours.astype(bf16), squares

    def attended(layer, i, ours, squares, previous):
        span = spans[i]
        across = send(ours, pipe_from(1 - layer))
        rest = (
            lax.rsqrt(squares / features + EPS),
            cosine[span],
            sine[span],
            bias[span],
            cached_key_rows[0, span],
            cached_value_rows[0, span],
        )
        heads = [None, None]
        heads[layer] = attention(layer, ours, *rest)
        heads[1 - layer] = attention(1 - layer, across, *rest)
        taken = send(heads[1 - layer], pipe_from(layer))
        shrunk = shrink(*heads, down, own_ids[span], jnp.where(p == layer, gate[span], 0.0))
        heads = jnp.where(p == layer, heads[layer], taken)
        load = jnp.concatenate([heads.reshape(-1, LANES), shrunk], axis=0)
        load = load if previous is None else after(load, previous)
        return load, exchange(jnp.broadcast_to(load[None], (16,) + load.shape), DP)

    def reduced(load, row_ids, weights, before):
        give = project_out(load, row_ids, weights, w_out[2], size, 2 * (1 - core))
        came = send(give, other_core).reshape(4, -1, block)
        keep = project_out(load, row_ids, weights, w_out[2], size, 2 * core)
        keep = keep.reshape(4, -1, block)
        before = before.reshape(8, -1, block)
        total = lax.dynamic_index_in_dim(before, core * 4 + x, 0, keepdims=False).astype(f32)

        def quarter_of(k):
            here = lax.dynamic_index_in_dim(keep, (x + k) % 4, 0, keepdims=False)
            there = lax.dynamic_index_in_dim(came, (x + k) % 4, 0, keepdims=False)
            return here.astype(f32) + there.astype(f32)

        parts = [send(quarter_of(k).astype(bf16), ring(k)) for k in (2, 1, 3)]
        total = total + quarter_of(0)
        for part in parts:
            total = total + part.astype(f32)
        return total.astype(bf16)

    def spread(total):
        total = exchange(jnp.broadcast_to(total[None], (4,) + total.shape), RING)
        total = total.reshape(-1, block)
        there = send(total, other_core)
        return jnp.concatenate(
            [jnp.where(core == 0, total, there), jnp.where(core == 0, there, total)], axis=0
        )

    w_out = []
    mine_in = in_half(p)
    for layer in range(2):
        weights = jnp.where(p == layer, mine_in, in_got)
        sums, loads = [], []
        got = None
        for i in range(PIECES):
            got, *found = summed(layer, i, weights, got)
            sums.append(found)
        for i in range(PIECES):
            ours, squares = sums[i]
            if i:
                ours = after(ours, load)
            load, got = attended(layer, i, ours, squares, loads[-1] if i else None)
            loads.append(got)
        state = [reduced(loads[i], ids[i], w_out[layer], state[i]) for i in range(PIECES)]
        if layer == 0:
            state = [spread(part) for part in state]

    total = state[0].reshape(4, half, block)
    pieces = []
    for m in range(4):
        other = m ^ y
        piece = lax.dynamic_index_in_dim(total, other % 2 * 2 + other // 2, 0, keepdims=False)
        pieces.append(
            send(
                piece,
                lambda z, y, p, u, c, m=m: (
                    2 * c + p,
                    2 * u + (m ^ y) % 2,
                    (m ^ y) // 2,
                    z // 2,
                    z % 2,
                ),
            )
        )
    odd = y % 2 == 1
    pieces = [jnp.where(odd, pieces[m ^ 1], pieces[m]) for m in range(4)]
    pieces = [jnp.where(p == 1, pieces[m ^ 2], pieces[m]) for m in range(4)]
    return jnp.concatenate(pieces, axis=1)


def solution(mesh):
    torus = Mesh(mesh.devices.reshape(4, 4, 2, 2, 2), AXES)
    heads = ("xl", "core")
    placed = (
        P(DP, heads),
        P("pipe", None),
        P("pipe", DP, heads),
        P("pipe", DP, heads),
        P("pipe", DP, heads),
        P("pipe", heads, DP),
        P("pipe", heads, None, None),
        P("pipe", None, None, heads),
        P("pipe", DP, None, heads),
        P("pipe", DP, None, heads),
        P(DP),
        P(),
        P(DP),
    )
    return jax.shard_map(
        on_device,
        mesh=torus,
        in_specs=placed,
        out_specs=P(("z", "y", "pipe"), heads),
        check_vma=False,
    )
```

time: 360 us -> 323 us (0.90)
  starting transfers between devices: 101 us -> 71.4 us
  matrix products: 19.8 us -> 3.22 us
  local copies, waits for them, and re-layouts: 43.8 us -> 28.3 us
  blocking collectives: 81.3 us -> 90.8 us
  Pallas kernels: 11 us -> 18.3 us
  other arithmetic: 18.6 us -> 23.2 us
    dot_general x8 -> x1, matrix products: 19.8 us -> 3.22 us  [summed(): parts = jnp.dot(state[i], weights, preferred_element_type=f32).astype(bf16)]
    ppermute x24 -> x27, waiting for transfers between devices: 34.2 us -> 50.1 us  [send(): return lax.ppermute(block, AXES, pairs)]
    ppermute x24 -> x27, starting transfers between devices: 76.6 us -> 61.1 us  [send(): return lax.ppermute(block, AXES, pairs)]
    all_to_all x4 -> x2, waiting for transfers between devices: 47.5 us -> 33.3 us  [exchange(): return lax.all_to_all(blocks, axes, 0, 0, tiled=True)]
    all_to_all x4 -> x2, starting transfers between devices: 23.9 us -> 10.3 us  [exchange(): return lax.all_to_all(blocks, axes, 0, 0, tiled=True)]
    another operation x4 -> x1, local copies, waits for them, and re-layouts: 9.8 us -> 0.02 us  [on_device(): turned = jnp.stack([turned[:, k * block:(k + 1) * block] for k in range(4)])]
    all_to_all x3 -> x4, blocking collectives: 81.3 us -> 90.8 us  [exchange(): return lax.all_to_all(blocks, axes, 0, 0, tiled=True)]
    pallas_call x4 -> x11, Pallas kernels: 11 us -> 18.3 us  [the longest x4 8.58 us: project_out(): pl.pallas_call(lambda *refs: project_out_kernel(rows, *refs), grid_spec=p...]
  transfers between devices with their start and end apart: 28 -> 29, of which waited for: 14 -> 17; matrix products, arithmetic and copies ran while one was open for 16% -> 9% of each run, Pallas kernels for 0% -> 3%
where the time goes in v1:
time: 323 us; the launch traced here: 319 us
  blocking collectives  90.8 us (28%)
  waiting for transfers between devices  83.4 us (26%)
  starting transfers between devices  71.4 us (22%)
  local copies, waits for them, and re-layouts  28.3 us (9%)
  other arithmetic  23.2 us (7%)
  Pallas kernels  18.3 us (6%)
    all_to_all x4, blocking collectives, exchange(): return lax.all_to_all(blocks, axes, 0, 0, tiled=True)  90.8 us
    ppermute x27, starting transfers between devices, send(): return lax.ppermute(block, AXES, pairs)  61.1 us
    ppermute x27, waiting for transfers between devices, send(): return lax.ppermute(block, AXES, pairs)  50.1 us
    all_to_all x2, waiting for transfers between devices, exchange(): return lax.all_to_all(blocks, axes, 0, 0, tiled=True)  33.3 us
    unnamed x83, local copies, waits for them, and re-layouts  17.7 us
    all_to_all x2, starting transfers between devices, exchange(): return lax.all_to_all(blocks, axes, 0, 0, tiled=True)  10.3 us
    pallas_call x4, Pallas kernels, project_out(): pl.pallas_call(lambda *refs: project_out_kernel(rows, *refs), grid_spec=p...  8.58 us
  transfers between devices with their start and end apart: 29, of which 17 were waited for; matrix products, arithmetic and copies ran while one was open for 9% of the time, Pallas kernels for 3%

profile of v1, /device:TPU:1, one launch (start us, length us, event | category | flops | bytes accessed | tf_op | source)
XLA Modules:
  0.0 319.4 jit_solution(4524230111227129053)
XLA Ops:
  1.6 4.9 %collective-permute-start = (bf16[80,2048]{1,0:T(8,128)(2,1)S(1)}, bf16[80,2048]{1,0:T(8,128)(2,1)S(1)}, u32[]{:S(2)}, u32[]{:S(2)}) collective-permute-start(bf16[80,2048]{1,0:T(8,128)(2,1)S(1)} %maximum_maximum_fusion), channel_id=1, source_target_pairs={{0,0},{1,32},{2,64},{3,96},{4,4},{5,36},{6,68},{7,100},{8,8},{9,40... | collective-permute-start | bytes 983048 | tf_op jit(solution)/shard_map/ppermute | solution.py:38
  12.3 4.9 %collective-permute-start.3 = (bf16[464,1280]{1,0:T(8,128)(2,1)}, bf16[464,1280]{1,0:T(8,128)(2,1)}, u32[]{:S(2)}, u32[]{:S(2)}) collective-permute-start(bf16[464,1280]{1,0:T(8,128)(2,1)} %slice.70), channel_id=1, source_target_pairs={{0,6},{1,7},{2,4},{3,5},{4,2},{5,3},{6,0},{7,1},{8,14},{9,15},{10,... | collective-permute-start | bytes 3563528 | tf_op jit(solution)/shard_map/ppermute | solution.py:38
  17.2 10.7 %all_to_all.30 = bf16[4,80,512]{2,1,0:T(8,128)(2,1)} all-to-all(bf16[4,80,512]{2,1,0:T(8,128)(2,1)S(1)} %pad_maximum_fusion.3), channel_id=1, replica_groups=mesh['z'=4,'y'=4,'pipe'=2,'xl'=2,'core'=2] {'y'}, dimensions={0} | all-to-all | bytes 655360 | tf_op jit(solution)/shard_map/all_to_all | solution.py:66
  28.2 5.3 %copy.33 = bf16[256,8,8,128]{3,1,2,0:T(8,128)(2,1)} copy(bf16[256,8,8,128]{3,2,1,0:T(8,128)(2,1)} %bitcast.121) | data formatting | bytes 8388608
  52.9 3.2 %convolution_convert_fusion = bf16[1024,1280]{1,0:T(8,128)(2,1)} fusion(bf16[1024,512]{1,0:T(8,128)(2,1)S(1)} %bitcast.124, bf16[512,1280]{1,0:T(8,128)(2,1)S(1)} %constant_dynamic-update-slice_fusion, pred[]{:T(512)S(6)} %eq.75, bf16[512,128]{1,0:T(8,128)(2,1)S(1)} %get-tuple-element.57, bf16[512,128]{1,0:T(8,128)(2,1)S(1)} %copy-done.33, ...), kind=kOutput, calls=%fused_computation.2 | convolution fusion | flops 1349386240 | bytes 6293505 | tf_op jit(solution)/shard_map/dot_general | solution.py:317
  57.9 5.7 %all-to-all-start.1 = ((bf16[16,64,1280]{2,1,0:T(8,128)(2,1)}), bf16[16,64,1280]{2,1,0:T(8,128)(2,1)}, u32[]{:S(2)}, u32[]{:S(2)}) async-start(bf16[16,64,1280]{2,1,0:T(8,128)(2,1)} %bitcast.122), calls=%async_computation.1 | async-start | bytes 5242880 | tf_op jit(solution)/shard_map/all_to_all | solution.py:66
  71.9 2.9 collective-permute-start.9
  74.8 15.3 %collective-permute-done.5 = bf16[1024,512]{1,0:T(8,128)(2,1)} collective-permute-done((bf16[1024,512]{1,0:T(8,128)(2,1)}, bf16[1024,512]{1,0:T(8,128)(2,1)}, u32[]{:S(2)}, u32[]{:S(2)}) %collective-permute-start.5) | collective-permute-done | bytes 1048608 | tf_op jit(solution)/shard_map/ppermute | solution.py:38
  95.1 6.4 %all-to-all-done.1 = bf16[16,64,1280]{2,1,0:T(8,128)(2,1)} async-done(((bf16[16,64,1280]{2,1,0:T(8,128)(2,1)}), bf16[16,64,1280]{2,1,0:T(8,128)(2,1)}, u32[]{:S(2)}, u32[]{:S(2)}) %all-to-all-start.1) | async-done | bytes 2621472 | tf_op jit(solution)/shard_map/all_to_all | solution.py:66
  105.1 5.9 %collective-permute-done.10.refs_0_ = bf16[64,1280]{1,0:T(8,128)(2,1)S(1)} collective-permute-done((bf16[64,1280]{1,0:T(8,128)(2,1)S(1)}, bf16[64,1280]{1,0:T(8,128)(2,1)S(1)}, u32[]{:S(2)}, u32[]{:S(2)}) %collective-permute-start.10) | collective-permute-done | bytes 163872 | tf_op jit(solution)/shard_map/ppermute | solution.py:38
  120.5 4.6 %all-to-all-start.2 = ((bf16[16,576,128]{2,1,0:T(8,128)(2,1)}), bf16[16,576,128]{2,1,0:T(8,128)(2,1)}, u32[]{:S(2)}, u32[]{:S(2)}) async-start(bf16[16,576,128]{2,1,0:T(8,128)(2,1)} %broadcast_in_dim.84), calls=%async_computation.2 | async-start | bytes 4718592 | tf_op jit(solution)/shard_map/all_to_all | solution.py:66
  126.0 26.9 %all-to-all-done.2.refs_1_ = bf16[16,576,128]{2,1,0:T(8,128)(2,1)} async-done(((bf16[16,576,128]{2,1,0:T(8,128)(2,1)}), bf16[16,576,128]{2,1,0:T(8,128)(2,1)}, u32[]{:S(2)}, u32[]{:S(2)}) %all-to-all-start.2) | async-done | bytes 2359328 | tf_op jit(solution)/shard_map/all_to_all | solution.py:66
  155.6 3.2 %shard_map.131 = bf16[512,512]{1,0:T(8,128)(2,1)} custom-call(s32[1]{0:T(128)} %bitcast.27.refs_0_, bf16[16,576,128]{2,1,0:T(8,128)(2,1)} %all-to-all-done.2.refs_1_, bf16[1024,128]{1,0:T(8,128)(2,1)S(1)} %broadcast_in_dim.86.refs_2_, bf16[1024,512]{1,0:T(8,128)(2,1)S(1)} %copy-done.10, bf16[1024,512]{1,0:T(8,128)(2,1)S(1)} %copy-done.6), custom_call_target="tpu_custom_call" | custom-call | flops 1000000000 | bytes 5000000 | tf_op jit(solution)/shard_map/pallas_call | solution.py:131
  158.8 6.5 %collective-permute-start.12 = (bf16[512,512]{1,0:T(8,128)(2,1)}, bf16[512,512]{1,0:T(8,128)(2,1)}, u32[]{:S(2)}, u32[]{:S(2)}) collective-permute-start(bf16[512,512]{1,0:T(8,128)(2,1)} %shard_map.131), channel_id=1, source_target_pairs={{0,1},{1,0},{2,3},{3,2},{4,5},{5,4},{6,7},{7,6},{8,9},{9,8},{10,11... | collective-permute-start | bytes 1572872 | tf_op jit(solution)/shard_map/ppermute | solution.py:38
  175.2 3.8 %collective-permute-done.13 = bf16[128,512]{1,0:T(8,128)(2,1)} collective-permute-done((bf16[128,512]{1,0:T(8,128)(2,1)}, bf16[128,512]{1,0:T(8,128)(2,1)}, u32[]{:S(2)}, u32[]{:S(2)}) %collective-permute-start.13) | collective-permute-done | bytes 131104 | tf_op jit(solution)/shard_map/ppermute | solution.py:38
  179.1 3.0 collective-permute-done.15
  183.4 12.2 %all_to_all.31 = bf16[4,128,512]{2,1,0:T(8,128)(2,1)S(1)} all-to-all(bf16[4,128,512]{2,1,0:T(8,128)(2,1)S(1)} %broadcast_in_dim.87), channel_id=1, replica_groups=mesh['z'=4,'y'=4,'pipe'=2,'xl'=2,'core'=2] {'pipe','xl'}, dimensions={0} | all-to-all | bytes 1048576 | tf_op jit(solution)/shard_map/all_to_all | solution.py:66
  201.5 37.2 %all_to_all.32 = bf16[16,656,128]{2,1,0:T(8,128)(2,1)S(1)} all-to-all(bf16[16,656,128]{2,1,0:T(8,128)(2,1)S(1)} %shard_map.132), channel_id=1, replica_groups=mesh['z'=4,'y'=4,'pipe'=2,'xl'=2,'core'=2] {'z','y'}, dimensions={0} | all-to-all | bytes 5373952 | tf_op jit(solution)/shard_map/all_to_all | solution.py:66
  251.3 3.5 %collective-permute-done.18 = bf16[8,64,128]{2,1,0:T(8,128)(2,1)S(1)} collective-permute-done((bf16[8,64,128]{2,1,0:T(8,128)(2,1)S(1)}, bf16[8,64,128]{2,1,0:T(8,128)(2,1)S(1)}, u32[]{:S(2)}, u32[]{:S(2)}) %collective-permute-start.18) | collective-permute-done | bytes 131104 | tf_op jit(solution)/shard_map/ppermute | solution.py:38
  255.3 30.8 %all_to_all.33.refs_1_ = bf16[16,576,128]{2,1,0:T(8,128)(2,1)S(1)} all-to-all(bf16[16,576,128]{2,1,0:T(8,128)(2,1)S(1)} %broadcast_in_dim.88), channel_id=1, replica_groups=mesh['z'=4,'y'=4,'pipe'=2,'xl'=2,'core'=2] {'z','y'}, dimensions={0} | all-to-all | bytes 4718592 | tf_op jit(solution)/shard_map/all_to_all | solution.py:66
  287.5 4.7 %collective-permute-start.19 = (bf16[512,512]{1,0:T(8,128)(2,1)S(1)}, bf16[512,512]{1,0:T(8,128)(2,1)S(1)}, u32[]{:S(2)}, u32[]{:S(2)}) collective-permute-start(bf16[512,512]{1,0:T(8,128)(2,1)S(1)} %shard_map.137), channel_id=1, source_target_pairs={{0,1},{1,0},{2,3},{3,2},{4,5},{5,4},{6,7},{7,6},{8,9},{9,8},{10,11... | collective-permute-start | bytes 1572872 | tf_op jit(solution)/shard_map/ppermute | solution.py:38
  295.5 4.7 %collective-permute-done.20 = bf16[128,512]{1,0:T(8,128)(2,1)S(1)} collective-permute-done((bf16[128,512]{1,0:T(8,128)(2,1)S(1)}, bf16[128,512]{1,0:T(8,128)(2,1)S(1)}, u32[]{:S(2)}, u32[]{:S(2)}) %collective-permute-start.20) | collective-permute-done | bytes 131104 | tf_op jit(solution)/shard_map/ppermute | solution.py:38
  300.7 3.0 collective-permute-done.21
  308.6 4.6 %collective-permute-start.24 = (bf16[32,512]{1,0:T(8,128)(2,1)S(1)}, bf16[32,512]{1,0:T(8,128)(2,1)S(1)}, u32[]{:S(2)}, u32[]{:S(2)}) collective-permute-start(bf16[32,512]{1,0:T(8,128)(2,1)S(1)} %get-tuple-element.65), channel_id=1, source_target_pairs={{0,4},{1,68},{2,20},{3,84},{4,36},{5,100},{6,52},{7,116},{8,12},{9... | collective-permute-start | bytes 98312 | tf_op jit(solution)/shard_map/ppermute | solution.py:38
  (195 shorter events, 104.8 us)
Async XLA Ops:
  1.6 15.5 %collective-permute-start = (bf16[80,2048]{1,0:T(8,128)(2,1)S(1)}, bf16[80,2048]{1,0:T(8,128)(2,1)S(1)}, u32[]{:S(2)}, u32[]{:S(2)}) collective-permute-start(bf16[80,2048]{1,0:T(8,128)(2,1)S(1)} %maximum_maximum_fusion), channel_id=1, source_target_pairs={{0,0},{1,32},{2,64},{3,96},{4,4},{5,36},{6,68},{7,100},{8,8},{9,40... | collective-permute-start | bytes 983048 | tf_op jit(solution)/shard_map/ppermute | solution.py:38
  12.3 31.5 %collective-permute-start.3 = (bf16[464,1280]{1,0:T(8,128)(2,1)}, bf16[464,1280]{1,0:T(8,128)(2,1)}, u32[]{:S(2)}, u32[]{:S(2)}) collective-permute-start(bf16[464,1280]{1,0:T(8,128)(2,1)} %slice.70), channel_id=1, source_target_pairs={{0,6},{1,7},{2,4},{3,5},{4,2},{5,3},{6,0},{7,1},{8,14},{9,15},{10,... | collective-permute-start | bytes 3563528 | tf_op jit(solution)/shard_map/ppermute | solution.py:38
  28.0 8.6 %collective-permute-start.1 = (bf16[4,80,512]{2,1,0:T(8,128)(2,1)}, bf16[4,80,512]{2,1,0:T(8,128)(2,1)}, u32[]{:S(2)}, u32[]{:S(2)}) collective-permute-start(bf16[4,80,512]{2,1,0:T(8,128)(2,1)} %all_to_all.30), channel_id=1, source_target_pairs={{0,2},{1,3},{2,0},{3,1},{4,6},{5,7},{6,4},{7,5},{8,10},{9,11},{10,... | collective-permute-start | bytes 983048 | tf_op jit(solution)/shard_map/ppermute | solution.py:38
  39.3 9.9 %collective-permute-start.2 = (bf16[2,4,80,512]{3,2,1,0:T(8,128)(2,1)}, bf16[2,4,80,512]{3,2,1,0:T(8,128)(2,1)}, u32[]{:S(2)}, u32[]{:S(2)}) collective-permute-start(bf16[2,4,80,512]{3,2,1,0:T(8,128)(2,1)} %pad_maximum_fusion.2), channel_id=1, source_target_pairs={{0,1},{1,0},{2,3},{3,2},{4,5},{5,4},{6,7},{7,6},{8,9},{9,8},{10,11... | collective-permute-start | bytes 1966088 | tf_op jit(solution)/shard_map/ppermute | solution.py:38
  56.1 12.2 %collective-permute-start.6 = (bf16[1024,512]{1,0:T(8,128)(2,1)S(1)}, bf16[1024,512]{1,0:T(8,128)(2,1)}, u32[]{:S(2)}, u32[]{:S(2)}) collective-permute-start(bf16[1024,512]{1,0:T(8,128)(2,1)S(1)} %constant_dynamic-slice_fusion.1), channel_id=1, source_target_pairs={{0,2},{4,6},{8,10},{12,14},{16,18},{20,22},{24,26},{28,30},{33,35}... | collective-permute-start | bytes 3145736 | tf_op jit(solution)/shard_map/ppermute | solution.py:38
  57.9 43.7 %all-to-all-start.1 = ((bf16[16,64,1280]{2,1,0:T(8,128)(2,1)}), bf16[16,64,1280]{2,1,0:T(8,128)(2,1)}, u32[]{:S(2)}, u32[]{:S(2)}) async-start(bf16[16,64,1280]{2,1,0:T(8,128)(2,1)} %bitcast.122), calls=%async_computation.1 | async-start | bytes 5242880 | tf_op jit(solution)/shard_map/all_to_all | solution.py:66
  63.7 8.2 %collective-permute-start.8 = (f32[1,64]{1,0:T(1,128)S(1)}, f32[1,64]{1,0:T(1,128)S(1)}, u32[]{:S(2)}, u32[]{:S(2)}) collective-permute-start(f32[1,64]{1,0:T(1,128)S(1)} %bitcast.137), channel_id=1, source_target_pairs={{0,2},{1,3},{2,0},{3,1},{4,6},{5,7},{6,4},{7,5},{8,10},{9,11},{10,... | collective-permute-start | bytes 776 | tf_op jit(solution)/shard_map/ppermute | solution.py:38
  66.4 23.7 %collective-permute-start.5 = (bf16[1024,512]{1,0:T(8,128)(2,1)}, bf16[1024,512]{1,0:T(8,128)(2,1)}, u32[]{:S(2)}, u32[]{:S(2)}) collective-permute-start(bf16[1024,512]{1,0:T(8,128)(2,1)} %get-tuple-element.22), channel_id=1, source_target_pairs={{0,6},{1,7},{2,4},{3,5},{4,2},{5,3},{6,0},{7,1},{8,14},{9,15},{10,... | collective-permute-start | bytes 3145736 | tf_op jit(solution)/shard_map/ppermute | solution.py:38
  69.6 23.2 %collective-permute-start.7 = (bf16[1024,512]{1,0:T(8,128)(2,1)S(1)}, bf16[1024,512]{1,0:T(8,128)(2,1)}, u32[]{:S(2)}, u32[]{:S(2)}) collective-permute-start(bf16[1024,512]{1,0:T(8,128)(2,1)S(1)} %broadcast_select_fusion.1), channel_id=1, source_target_pairs={{0,1},{2,3},{4,5},{6,7},{8,9},{10,11},{12,13},{14,15},{16,17},{18,... | collective-permute-start | bytes 3145736 | tf_op jit(solution)/shard_map/ppermute | solution.py:38
  71.9 33.1 %collective-permute-start.9 = (f32[1,64]{1,0:T(1,128)S(1)}, f32[1,64]{1,0:T(1,128)S(1)}, u32[]{:S(2)}, u32[]{:S(2)}) collective-permute-start(f32[1,64]{1,0:T(1,128)S(1)} %bitcast_add_fusion.2), channel_id=1, source_target_pairs={{0,1},{1,0},{2,3},{3,2},{4,5},{5,4},{6,7},{7,6},{8,9},{9,8},{10,11... | collective-permute-start | bytes 776 | tf_op jit(solution)/shard_map/ppermute | solution.py:38
  103.7 7.3 %collective-permute-start.10 = (bf16[64,1280]{1,0:T(8,128)(2,1)S(1)}, bf16[64,1280]{1,0:T(8,128)(2,1)S(1)}, u32[]{:S(2)}, u32[]{:S(2)}) collective-permute-start(bf16[64,1280]{1,0:T(8,128)(2,1)S(1)} %reduce_sum.39.refs_0_), channel_id=1, source_target_pairs={{4,2},{5,3},{6,0},{7,1},{12,10},{13,11},{14,8},{15,9},{20,18},{21,... | collective-permute-start | bytes 491528 | tf_op jit(solution)/shard_map/ppermute | solution.py:38
  120.5 32.4 %all-to-all-start.2 = ((bf16[16,576,128]{2,1,0:T(8,128)(2,1)}), bf16[16,576,128]{2,1,0:T(8,128)(2,1)}, u32[]{:S(2)}, u32[]{:S(2)}) async-start(bf16[16,576,128]{2,1,0:T(8,128)(2,1)} %broadcast_in_dim.84), calls=%async_computation.2 | async-start | bytes 4718592 | tf_op jit(solution)/shard_map/all_to_all | solution.py:66
  158.8 11.5 %collective-permute-start.12 = (bf16[512,512]{1,0:T(8,128)(2,1)}, bf16[512,512]{1,0:T(8,128)(2,1)}, u32[]{:S(2)}, u32[]{:S(2)}) collective-permute-start(bf16[512,512]{1,0:T(8,128)(2,1)} %shard_map.131), channel_id=1, source_target_pairs={{0,1},{1,0},{2,3},{3,2},{4,5},{5,4},{6,7},{7,6},{8,9},{9,8},{10,11... | collective-permute-start | bytes 1572872 | tf_op jit(solution)/shard_map/ppermute | solution.py:38
  172.1 6.9 %collective-permute-start.13 = (bf16[128,512]{1,0:T(8,128)(2,1)}, bf16[128,512]{1,0:T(8,128)(2,1)}, u32[]{:S(2)}, u32[]{:S(2)}) collective-permute-start(bf16[128,512]{1,0:T(8,128)(2,1)} %get-tuple-element.42), channel_id=1, source_target_pairs={{0,4},{1,5},{2,6},{3,7},{4,0},{5,1},{6,2},{7,3},{8,12},{9,13},{10,... | collective-permute-start | bytes 393224 | tf_op jit(solution)/shard_map/ppermute | solution.py:38
  173.6 8.4 %collective-permute-start.15 = (bf16[128,512]{1,0:T(8,128)(2,1)}, bf16[128,512]{1,0:T(8,128)(2,1)}, u32[]{:S(2)}, u32[]{:S(2)}) collective-permute-start(bf16[128,512]{1,0:T(8,128)(2,1)} %get-tuple-element.43), channel_id=1, source_target_pairs={{0,6},{1,7},{2,0},{3,1},{4,2},{5,3},{6,4},{7,5},{8,14},{9,15},{10,... | collective-permute-start | bytes 393224 | tf_op jit(solution)/shard_map/ppermute | solution.py:38
  174.9 7.2 %collective-permute-start.14 = (bf16[128,512]{1,0:T(8,128)(2,1)}, bf16[128,512]{1,0:T(8,128)(2,1)}, u32[]{:S(2)}, u32[]{:S(2)}) collective-permute-start(bf16[128,512]{1,0:T(8,128)(2,1)} %get-tuple-element.44), channel_id=1, source_target_pairs={{0,2},{1,3},{2,4},{3,5},{4,6},{5,7},{6,0},{7,1},{8,10},{9,11},{10,... | collective-permute-start | bytes 393224 | tf_op jit(solution)/shard_map/ppermute | solution.py:38
  247.5 7.3 %collective-permute-start.18 = (bf16[8,64,128]{2,1,0:T(8,128)(2,1)S(1)}, bf16[8,64,128]{2,1,0:T(8,128)(2,1)S(1)}, u32[]{:S(2)}, u32[]{:S(2)}) collective-permute-start(bf16[8,64,128]{2,1,0:T(8,128)(2,1)S(1)} %shard_map.134.low_ref), channel_id=1, source_target_pairs={{4,2},{5,3},{6,0},{7,1},{12,10},{13,11},{14,8},{15,9},{20,18},{21,... | collective-permute-start | bytes 393224 | tf_op jit(solution)/shard_map/ppermute | solution.py:38
  287.5 6.3 %collective-permute-start.19 = (bf16[512,512]{1,0:T(8,128)(2,1)S(1)}, bf16[512,512]{1,0:T(8,128)(2,1)S(1)}, u32[]{:S(2)}, u32[]{:S(2)}) collective-permute-start(bf16[512,512]{1,0:T(8,128)(2,1)S(1)} %shard_map.137), channel_id=1, source_target_pairs={{0,1},{1,0},{2,3},{3,2},{4,5},{5,4},{6,7},{7,6},{8,9},{9,8},{10,11... | collective-permute-start | bytes 1572872 | tf_op jit(solution)/shard_map/ppermute | solution.py:38
  293.9 6.3 %collective-permute-start.20 = (bf16[128,512]{1,0:T(8,128)(2,1)S(1)}, bf16[128,512]{1,0:T(8,128)(2,1)S(1)}, u32[]{:S(2)}, u32[]{:S(2)}) collective-permute-start(bf16[128,512]{1,0:T(8,128)(2,1)S(1)} %get-tuple-element.37), channel_id=1, source_target_pairs={{0,4},{1,5},{2,6},{3,7},{4,0},{5,1},{6,2},{7,3},{8,12},{9,13},{10,... | collective-permute-start | bytes 393224 | tf_op jit(solution)/shard_map/ppermute | solution.py:38
  294.0 6.7 %collective-permute-start.22 = (bf16[128,512]{1,0:T(8,128)(2,1)S(1)}, bf16[128,512]{1,0:T(8,128)(2,1)S(1)}, u32[]{:S(2)}, u32[]{:S(2)}) collective-permute-start(bf16[128,512]{1,0:T(8,128)(2,1)S(1)} %get-tuple-element.38), channel_id=1, source_target_pairs={{0,6},{1,7},{2,0},{3,1},{4,2},{5,3},{6,4},{7,5},{8,14},{9,15},{10,... | collective-permute-start | bytes 393224 | tf_op jit(solution)/shard_map/ppermute | solution.py:38
  294.5 9.2 %collective-permute-start.21 = (bf16[128,512]{1,0:T(8,128)(2,1)S(1)}, bf16[128,512]{1,0:T(8,128)(2,1)S(1)}, u32[]{:S(2)}, u32[]{:S(2)}) collective-permute-start(bf16[128,512]{1,0:T(8,128)(2,1)S(1)} %get-tuple-element.39), channel_id=1, source_target_pairs={{0,2},{1,3},{2,4},{3,5},{4,6},{5,7},{6,0},{7,1},{8,10},{9,11},{10,... | collective-permute-start | bytes 393224 | tf_op jit(solution)/shard_map/ppermute | solution.py:38
  304.8 10.1 %collective-permute-start.25 = (bf16[32,512]{1,0:T(8,128)(2,1)S(1)}, bf16[32,512]{1,0:T(8,128)(2,1)S(1)}, u32[]{:S(2)}, u32[]{:S(2)}) collective-permute-start(bf16[32,512]{1,0:T(8,128)(2,1)S(1)} %get-tuple-element.63), channel_id=1, source_target_pairs={{0,8},{1,72},{2,24},{3,88},{4,40},{5,104},{6,56},{7,120},{8,0},{9,... | collective-permute-start | bytes 98312 | tf_op jit(solution)/shard_map/ppermute | solution.py:38
  305.8 9.0 %collective-permute-start.26 = (bf16[32,512]{1,0:T(8,128)(2,1)S(1)}, bf16[32,512]{1,0:T(8,128)(2,1)S(1)}, u32[]{:S(2)}, u32[]{:S(2)}) collective-permute-start(bf16[32,512]{1,0:T(8,128)(2,1)S(1)} %get-tuple-element.64), channel_id=1, source_target_pairs={{0,0},{1,64},{2,16},{3,80},{4,32},{5,96},{6,48},{7,112},{8,8},{9,7... | collective-permute-start | bytes 98312 | tf_op jit(solution)/shard_map/ppermute | solution.py:38
  308.6 7.8 %collective-permute-start.24 = (bf16[32,512]{1,0:T(8,128)(2,1)S(1)}, bf16[32,512]{1,0:T(8,128)(2,1)S(1)}, u32[]{:S(2)}, u32[]{:S(2)}) collective-permute-start(bf16[32,512]{1,0:T(8,128)(2,1)S(1)} %get-tuple-element.65), channel_id=1, source_target_pairs={{0,4},{1,68},{2,20},{3,84},{4,36},{5,100},{6,52},{7,116},{8,12},{9... | collective-permute-start | bytes 98312 | tf_op jit(solution)/shard_map/ppermute | solution.py:38
  (45 other events, 339.9 us)

commit v2 on v1

--- a/solution.py
+++ b/solution.py
@@ -124,7 +124,7 @@
     out_ref[...] = total.astype(bf16)
 
 
-def project_out(load, ids, weights, up, rows, first, steps=2, groups=4):
+def project_out(load, ids, weights, up, rows, first, megabytes, steps=2, groups=4):
     count, length, _ = load.shape
     depth, width = weights.shape
     tile = groups * rows
@@ -142,7 +142,7 @@
             out_specs=pl.BlockSpec((tile, width), lambda i, f: (i, 0)),
         ),
         out_shape=jax.ShapeDtypeStruct((steps * tile, width), bf16),
-        compiler_params=pltpu.CompilerParams(vmem_limit_bytes=32 * 1024 * 1024),
+        compiler_params=pltpu.CompilerParams(vmem_limit_bytes=megabytes * 1024 * 1024),
         cost_estimate=pl.CostEstimate(flops=10**9, bytes_accessed=5 * 10**6, transcendentals=0),
     )(first.astype(jnp.int32).reshape(1), load, ids, weights, up)
 
@@ -199,25 +199,27 @@
     )(x, *rest)
 
 
-def shrink_kernel(low_ref, high_ref, down_ref, ids_ref, gate_ref, out_ref):
-    flat = [ref[j] for ref in (low_ref, high_ref) for j in range(ref.shape[0])]
-    product = jnp.dot(jnp.concatenate(flat, axis=1), down_ref[...], preferred_element_type=f32)
+def shrink_kernel(g, heads_ref, down_ref, ids_ref, gate_ref, out_ref):
+    flat = jnp.concatenate([heads_ref[j] for j in range(heads_ref.shape[0])], axis=1)
+    depth = flat.shape[1]
+    rows = slice(g * depth, (g + 1) * depth)
+    product = jnp.dot(flat, down_ref[rows], preferred_element_type=f32)
     ids = ids_ref[...]
     total = jnp.zeros(ids.shape, f32)
     for a in range(ADAPTERS):
         total = total + jnp.where(ids == a, product[:, a * RANK : (a + 1) * RANK], 0.0)
-    out_ref[...] = (total * gate_ref[...]).astype(bf16)
-
-
-def shrink(low, high, down, ids, gate):
+    out_ref[...] = total * gate_ref[...]
+
+
+def shrink(g, heads, down, ids, gate):
     return pl.pallas_call(
-        shrink_kernel,
-        in_specs=[pl.BlockSpec(memory_space=pltpu.VMEM)] * 5,
+        lambda *refs: shrink_kernel(g, *refs),
+        in_specs=[pl.BlockSpec(memory_space=pltpu.VMEM)] * 4,
         out_specs=pl.BlockSpec(memory_space=pltpu.VMEM),
-        out_shape=jax.ShapeDtypeStruct(ids.shape, bf16),
+        out_shape=jax.ShapeDtypeStruct(ids.shape, f32),
         compiler_params=pltpu.CompilerParams(vmem_limit_bytes=40 * 1024 * 1024),
         cost_estimate=pl.CostEstimate(flops=10**9, bytes_accessed=5 * 10**6, transcendentals=0),
-    )(low, high, down, ids, gate)
+    )(heads, down, ids, gate)
 
 
 def on_device(
@@ -321,7 +323,7 @@
             w_out.extend(later_weights(parts))
         parts = exchange(parts, DP)
         if layer == 0 and i == 0:
-            parts, *w_out[:] = lax.optimization_barrier((parts, *w_out))
+            parts, ids[:], *w_out[:] = lax.optimization_barrier((parts, ids, *w_out))
         sums = jnp.sum(parts.astype(f32), axis=0)
         if layer == 0:
             return parts, sums.astype(bf16), square[spans[i]]
@@ -342,18 +344,21 @@
         )
         heads = [None, None]
         heads[layer] = attention(layer, ours, *rest)
+        scale = jnp.where(p == layer, gate[span], 0.0)
+        shrunk = shrink(layer, heads[layer], down, own_ids[span], scale)
+        across, heads[layer], shrunk = lax.optimization_barrier((across, heads[layer], shrunk))
         heads[1 - layer] = attention(1 - layer, across, *rest)
         taken = send(heads[1 - layer], pipe_from(layer))
-        shrunk = shrink(*heads, down, own_ids[span], jnp.where(p == layer, gate[span], 0.0))
+        shrunk = shrunk + shrink(1 - layer, heads[1 - layer], down, own_ids[span], scale)
         heads = jnp.where(p == layer, heads[layer], taken)
-        load = jnp.concatenate([heads.reshape(-1, LANES), shrunk], axis=0)
+        load = jnp.concatenate([heads.reshape(-1, LANES), shrunk.astype(bf16)], axis=0)
         load = load if previous is None else after(load, previous)
         return load, exchange(jnp.broadcast_to(load[None], (16,) + load.shape), DP)
 
-    def reduced(load, row_ids, weights, before):
-        give = project_out(load, row_ids, weights, w_out[2], size, 2 * (1 - core))
+    def reduced(load, row_ids, weights, before, megabytes):
+        give = project_out(load, row_ids, weights, w_out[2], size, 2 * (1 - core), megabytes)
         came = send(give, other_core).reshape(4, -1, block)
-        keep = project_out(load, row_ids, weights, w_out[2], size, 2 * core)
+        keep = project_out(load, row_ids, weights, w_out[2], size, 2 * core, megabytes)
         keep = keep.reshape(4, -1, block)
         before = before.reshape(8, -1, block)
         total = lax.dynamic_index_in_dim(before, core * 4 + x, 0, keepdims=False).astype(f32)
@@ -392,7 +397,8 @@
                 ours = after(ours, load)
             load, got = attended(layer, i, ours, squares, loads[-1] if i else None)
             loads.append(got)
-        state = [reduced(loads[i], ids[i], w_out[layer], state[i]) for i in range(PIECES)]
+        room = 56 if layer == 0 else 32
+        state = [reduced(loads[i], ids[i], w_out[layer], state[i], room) for i in range(PIECES)]
         if layer == 0:
             state = [spread(part) for part in state]
 

time: 323 us -> 322 us (level)
  starting transfers between devices: 71.4 us -> 75.2 us
  waiting for transfers between devices: 83.4 us -> 79.7 us
  local copies, waits for them, and re-layouts: 28.3 us -> 24.8 us
    all_to_all x2, starting transfers between devices: 10.3 us -> 14.7 us  [exchange(): return lax.all_to_all(blocks, axes, 0, 0, tiled=True)]
    unnamed x83 -> x65, local copies, waits for them, and re-layouts: 17.7 us -> 13.5 us
  transfers between devices with their start and end apart: 29 -> 29, of which waited for: 17 -> 17; matrix products, arithmetic and copies ran while one was open for 9% -> 8% of each run, Pallas kernels for 3% -> 3%
where the time goes in v2:
time: 322 us; the launch traced here: 318 us
  blocking collectives  91.1 us (28%)
  waiting for transfers between devices  79.7 us (25%)
  starting transfers between devices  75.2 us (23%)
  local copies, waits for them, and re-layouts  24.8 us (8%)
  other arithmetic  22.5 us (7%)
  Pallas kernels  20.6 us (6%)
  matrix products  3.3 us (1%)
    all_to_all x4, blocking collectives, exchange(): return lax.all_to_all(blocks, axes, 0, 0, tiled=True)  91.1 us
    ppermute x27, starting transfers between devices, send(): return lax.ppermute(block, AXES, pairs)  60.5 us
    ppermute x27, waiting for transfers between devices, send(): return lax.ppermute(block, AXES, pairs)  47.6 us
    all_to_all x2, waiting for transfers between devices, exchange(): return lax.all_to_all(blocks, axes, 0, 0, tiled=True)  32.1 us
    all_to_all x2, starting transfers between devices, exchange(): return lax.all_to_all(blocks, axes, 0, 0, tiled=True)  14.7 us
    unnamed x65, local copies, waits for them, and re-layouts  13.5 us
    pallas_call x4, Pallas kernels, project_out(): pl.pallas_call(lambda *refs: project_out_kernel(rows, *refs), grid_spec=p...  10.7 us
  transfers between devices with their start and end apart: 29, of which 17 were waited for; matrix products, arithmetic and copies ran while one was open for 8% of the time, Pallas kernels for 3%

profile of v2, /device:TPU:1, one launch (start us, length us, event | category | flops | bytes accessed | tf_op | source)
XLA Modules:
  0.0 317.9 jit_solution(3560257156494675684)
XLA Ops:
  1.6 4.9 %collective-permute-start = (bf16[80,2048]{1,0:T(8,128)(2,1)S(1)}, bf16[80,2048]{1,0:T(8,128)(2,1)S(1)}, u32[]{:S(2)}, u32[]{:S(2)}) collective-permute-start(bf16[80,2048]{1,0:T(8,128)(2,1)S(1)} %maximum_maximum_fusion), channel_id=1, source_target_pairs={{0,0},{1,32},{2,64},{3,96},{4,4},{5,36},{6,68},{7,100},{8,8},{9,40... | collective-permute-start | bytes 983048 | tf_op jit(solution)/shard_map/ppermute | solution.py:38
  12.2 4.9 %collective-permute-start.3 = (bf16[464,1280]{1,0:T(8,128)(2,1)}, bf16[464,1280]{1,0:T(8,128)(2,1)}, u32[]{:S(2)}, u32[]{:S(2)}) collective-permute-start(bf16[464,1280]{1,0:T(8,128)(2,1)} %slice.70), channel_id=1, source_target_pairs={{0,6},{1,7},{2,4},{3,5},{4,2},{5,3},{6,0},{7,1},{8,14},{9,15},{10,... | collective-permute-start | bytes 3563528 | tf_op jit(solution)/shard_map/ppermute | solution.py:38
  17.2 10.7 %all_to_all.30 = bf16[4,80,512]{2,1,0:T(8,128)(2,1)} all-to-all(bf16[4,80,512]{2,1,0:T(8,128)(2,1)S(1)} %pad_maximum_fusion.3), channel_id=1, replica_groups=mesh['z'=4,'y'=4,'pipe'=2,'xl'=2,'core'=2] {'y'}, dimensions={0} | all-to-all | bytes 655360 | tf_op jit(solution)/shard_map/all_to_all | solution.py:66
  28.2 5.3 %copy.33 = bf16[256,8,8,128]{3,1,2,0:T(8,128)(2,1)} copy(bf16[256,8,8,128]{3,2,1,0:T(8,128)(2,1)} %bitcast.121) | data formatting | bytes 8388608
  52.8 3.3 %convolution_convert_fusion = bf16[1024,1280]{1,0:T(8,128)(2,1)} fusion(bf16[1024,512]{1,0:T(8,128)(2,1)S(1)} %bitcast.126, bf16[512,1280]{1,0:T(8,128)(2,1)S(1)} %constant_dynamic-update-slice_fusion, pred[]{:T(512)S(6)} %eq.75, bf16[512,128]{1,0:T(8,128)(2,1)S(1)} %get-tuple-element.71, bf16[512,128]{1,0:T(8,128)(2,1)S(1)} %copy-done.24, ...), kind=kOutput, calls=%fused_computation.2 | convolution fusion | flops 1349386240 | bytes 6293505 | tf_op jit(solution)/shard_map/dot_general | solution.py:319
  58.1 8.0 %all-to-all-start.1 = ((bf16[16,64,1280]{2,1,0:T(8,128)(2,1)}), bf16[16,64,1280]{2,1,0:T(8,128)(2,1)}, u32[]{:S(2)}, u32[]{:S(2)}) async-start(bf16[16,64,1280]{2,1,0:T(8,128)(2,1)} %bitcast.122), calls=%async_computation.1 | async-start | bytes 5242880 | tf_op jit(solution)/shard_map/all_to_all | solution.py:66
  75.8 14.5 %collective-permute-done.5 = bf16[1024,512]{1,0:T(8,128)(2,1)} collective-permute-done((bf16[1024,512]{1,0:T(8,128)(2,1)}, bf16[1024,512]{1,0:T(8,128)(2,1)}, u32[]{:S(2)}, u32[]{:S(2)}) %collective-permute-start.5) | collective-permute-done | bytes 1048608 | tf_op jit(solution)/shard_map/ppermute | solution.py:38
  95.3 4.3 %all-to-all-done.1 = bf16[16,64,1280]{2,1,0:T(8,128)(2,1)} async-done(((bf16[16,64,1280]{2,1,0:T(8,128)(2,1)}), bf16[16,64,1280]{2,1,0:T(8,128)(2,1)}, u32[]{:S(2)}, u32[]{:S(2)}) %all-to-all-start.1) | async-done | bytes 2621472 | tf_op jit(solution)/shard_map/all_to_all | solution.py:66
  111.9 3.9 %collective-permute-start.11 = (bf16[8,64,128]{2,1,0:T(8,128)(2,1)S(1)}, bf16[8,64,128]{2,1,0:T(8,128)(2,1)S(1)}, u32[]{:S(2)}, u32[]{:S(2)}) collective-permute-start(bf16[8,64,128]{2,1,0:T(8,128)(2,1)S(1)} %shard_map.129.refs_0_), channel_id=1, source_target_pairs={{0,6},{1,7},{2,4},{3,5},{8,14},{9,15},{10,12},{11,13},{16,22},{17,... | collective-permute-start | bytes 393224 | tf_op jit(solution)/shard_map/ppermute | solution.py:38
  119.5 6.7 %all-to-all-start.2 = ((bf16[16,576,128]{2,1,0:T(8,128)(2,1)}), bf16[16,576,128]{2,1,0:T(8,128)(2,1)}, u32[]{:S(2)}, u32[]{:S(2)}) async-start(bf16[16,576,128]{2,1,0:T(8,128)(2,1)} %broadcast_in_dim.86), calls=%async_computation.2 | async-start | bytes 4718592 | tf_op jit(solution)/shard_map/all_to_all | solution.py:66
  126.2 27.8 %all-to-all-done.2.refs_1_ = bf16[16,576,128]{2,1,0:T(8,128)(2,1)} async-done(((bf16[16,576,128]{2,1,0:T(8,128)(2,1)}), bf16[16,576,128]{2,1,0:T(8,128)(2,1)}, u32[]{:S(2)}, u32[]{:S(2)}) %all-to-all-start.2) | async-done | bytes 2359328 | tf_op jit(solution)/shard_map/all_to_all | solution.py:66
  153.9 3.9 %shard_map.132 = bf16[512,512]{1,0:T(8,128)(2,1)} custom-call(s32[1]{0:T(128)} %bitcast.27.refs_0_, bf16[16,576,128]{2,1,0:T(8,128)(2,1)} %all-to-all-done.2.refs_1_, bf16[1024,128]{1,0:T(8,128)(2,1)} %broadcast_in_dim.48.refs_2_, bf16[1024,512]{1,0:T(8,128)(2,1)} %get-tuple-element.37.refs_3_, bf16[1024,512]{1,0:T(8,128)(2,1)} %broadcast_select_fusion.2.refs_4_), custom_call_target="tpu_custom_call" | custom-call | flops 1000000000 | bytes 5000000 | tf_op jit(solution)/shard_map/pallas_call | solution.py:131
  157.8 6.5 %collective-permute-start.12 = (bf16[512,512]{1,0:T(8,128)(2,1)}, bf16[512,512]{1,0:T(8,128)(2,1)S(1)}, u32[]{:S(2)}, u32[]{:S(2)}) collective-permute-start(bf16[512,512]{1,0:T(8,128)(2,1)} %shard_map.132), channel_id=1, source_target_pairs={{0,1},{1,0},{2,3},{3,2},{4,5},{5,4},{6,7},{7,6},{8,9},{9,8},{10,11... | collective-permute-start | bytes 1572872 | tf_op jit(solution)/shard_map/ppermute | solution.py:38
  164.3 3.9 %shard_map.131 = bf16[512,512]{1,0:T(8,128)(2,1)} custom-call(s32[1]{0:T(128)} %bitcast.10.refs_0_, bf16[16,576,128]{2,1,0:T(8,128)(2,1)} %all-to-all-done.2.refs_1_, bf16[1024,128]{1,0:T(8,128)(2,1)} %broadcast_in_dim.48.refs_2_, bf16[1024,512]{1,0:T(8,128)(2,1)} %get-tuple-element.37.refs_3_, bf16[1024,512]{1,0:T(8,128)(2,1)} %broadcast_select_fusion.2.refs_4_), custom_call_target="tpu_custom_call" | custom-call | flops 1000000000 | bytes 5000000 | tf_op jit(solution)/shard_map/pallas_call | solution.py:131
  177.0 4.0 %collective-permute-done.15 = bf16[128,512]{1,0:T(8,128)(2,1)} collective-permute-done((bf16[128,512]{1,0:T(8,128)(2,1)}, bf16[128,512]{1,0:T(8,128)(2,1)}, u32[]{:S(2)}, u32[]{:S(2)}) %collective-permute-start.15) | collective-permute-done | bytes 131104 | tf_op jit(solution)/shard_map/ppermute | solution.py:38
  182.3 11.8 %all_to_all.31 = bf16[4,128,512]{2,1,0:T(8,128)(2,1)S(1)} all-to-all(bf16[4,128,512]{2,1,0:T(8,128)(2,1)S(1)} %broadcast_in_dim.87), channel_id=1, replica_groups=mesh['z'=4,'y'=4,'pipe'=2,'xl'=2,'core'=2] {'pipe','xl'}, dimensions={0} | all-to-all | bytes 1048576 | tf_op jit(solution)/shard_map/all_to_all | solution.py:66
  200.0 37.2 %all_to_all.32 = bf16[16,656,128]{2,1,0:T(8,128)(2,1)S(1)} all-to-all(bf16[16,656,128]{2,1,0:T(8,128)(2,1)S(1)} %shard_map.133), channel_id=1, replica_groups=mesh['z'=4,'y'=4,'pipe'=2,'xl'=2,'core'=2] {'z','y'}, dimensions={0} | all-to-all | bytes 5373952 | tf_op jit(solution)/shard_map/all_to_all | solution.py:66
  237.9 3.1 collective-permute-start.17
  247.9 5.6 %collective-permute-done.18 = bf16[8,64,128]{2,1,0:T(8,128)(2,1)S(1)} collective-permute-done((bf16[8,64,128]{2,1,0:T(8,128)(2,1)S(1)}, bf16[8,64,128]{2,1,0:T(8,128)(2,1)S(1)}, u32[]{:S(2)}, u32[]{:S(2)}) %collective-permute-start.18) | collective-permute-done | bytes 131104 | tf_op jit(solution)/shard_map/ppermute | solution.py:38
  254.0 31.4 %all_to_all.33.refs_1_ = bf16[16,576,128]{2,1,0:T(8,128)(2,1)S(1)} all-to-all(bf16[16,576,128]{2,1,0:T(8,128)(2,1)S(1)} %broadcast_in_dim.88), channel_id=1, replica_groups=mesh['z'=4,'y'=4,'pipe'=2,'xl'=2,'core'=2] {'z','y'}, dimensions={0} | all-to-all | bytes 4718592 | tf_op jit(solution)/shard_map/all_to_all | solution.py:66
  286.9 4.0 %collective-permute-start.19 = (bf16[512,512]{1,0:T(8,128)(2,1)S(1)}, bf16[512,512]{1,0:T(8,128)(2,1)S(1)}, u32[]{:S(2)}, u32[]{:S(2)}) collective-permute-start(bf16[512,512]{1,0:T(8,128)(2,1)S(1)} %shard_map.139), channel_id=1, source_target_pairs={{0,1},{1,0},{2,3},{3,2},{4,5},{5,4},{6,7},{7,6},{8,9},{9,8},{10,11... | collective-permute-start | bytes 1572872 | tf_op jit(solution)/shard_map/ppermute | solution.py:38
  294.1 4.7 %collective-permute-done.20 = bf16[128,512]{1,0:T(8,128)(2,1)S(1)} collective-permute-done((bf16[128,512]{1,0:T(8,128)(2,1)S(1)}, bf16[128,512]{1,0:T(8,128)(2,1)S(1)}, u32[]{:S(2)}, u32[]{:S(2)}) %collective-permute-start.20) | collective-permute-done | bytes 131104 | tf_op jit(solution)/shard_map/ppermute | solution.py:38
  298.8 3.5 %collective-permute-done.21 = bf16[128,512]{1,0:T(8,128)(2,1)S(1)} collective-permute-done((bf16[128,512]{1,0:T(8,128)(2,1)S(1)}, bf16[128,512]{1,0:T(8,128)(2,1)S(1)}, u32[]{:S(2)}, u32[]{:S(2)}) %collective-permute-start.21) | collective-permute-done | bytes 131104 | tf_op jit(solution)/shard_map/ppermute | solution.py:38
  307.2 4.6 %collective-permute-start.24 = (bf16[32,512]{1,0:T(8,128)(2,1)S(1)}, bf16[32,512]{1,0:T(8,128)(2,1)S(1)}, u32[]{:S(2)}, u32[]{:S(2)}) collective-permute-start(bf16[32,512]{1,0:T(8,128)(2,1)S(1)} %get-tuple-element.79), channel_id=1, source_target_pairs={{0,4},{1,68},{2,20},{3,84},{4,36},{5,100},{6,52},{7,116},{8,12},{9... | collective-permute-start | bytes 98312 | tf_op jit(solution)/shard_map/ppermute | solution.py:38
  (181 shorter events, 98.9 us)
Async XLA Ops:
  1.6 15.5 %collective-permute-start = (bf16[80,2048]{1,0:T(8,128)(2,1)S(1)}, bf16[80,2048]{1,0:T(8,128)(2,1)S(1)}, u32[]{:S(2)}, u32[]{:S(2)}) collective-permute-start(bf16[80,2048]{1,0:T(8,128)(2,1)S(1)} %maximum_maximum_fusion), channel_id=1, source_target_pairs={{0,0},{1,32},{2,64},{3,96},{4,4},{5,36},{6,68},{7,100},{8,8},{9,40... | collective-permute-start | bytes 983048 | tf_op jit(solution)/shard_map/ppermute | solution.py:38
  12.2 31.5 %collective-permute-start.3 = (bf16[464,1280]{1,0:T(8,128)(2,1)}, bf16[464,1280]{1,0:T(8,128)(2,1)}, u32[]{:S(2)}, u32[]{:S(2)}) collective-permute-start(bf16[464,1280]{1,0:T(8,128)(2,1)} %slice.70), channel_id=1, source_target_pairs={{0,6},{1,7},{2,4},{3,5},{4,2},{5,3},{6,0},{7,1},{8,14},{9,15},{10,... | collective-permute-start | bytes 3563528 | tf_op jit(solution)/shard_map/ppermute | solution.py:38
  27.9 8.6 %collective-permute-start.1 = (bf16[4,80,512]{2,1,0:T(8,128)(2,1)}, bf16[4,80,512]{2,1,0:T(8,128)(2,1)}, u32[]{:S(2)}, u32[]{:S(2)}) collective-permute-start(bf16[4,80,512]{2,1,0:T(8,128)(2,1)} %all_to_all.30), channel_id=1, source_target_pairs={{0,2},{1,3},{2,0},{3,1},{4,6},{5,7},{6,4},{7,5},{8,10},{9,11},{10,... | collective-permute-start | bytes 983048 | tf_op jit(solution)/shard_map/ppermute | solution.py:38
  39.3 10.0 %collective-permute-start.2 = (bf16[2,4,80,512]{3,2,1,0:T(8,128)(2,1)}, bf16[2,4,80,512]{3,2,1,0:T(8,128)(2,1)}, u32[]{:S(2)}, u32[]{:S(2)}) collective-permute-start(bf16[2,4,80,512]{3,2,1,0:T(8,128)(2,1)} %pad_maximum_fusion.2), channel_id=1, source_target_pairs={{0,1},{1,0},{2,3},{3,2},{4,5},{5,4},{6,7},{7,6},{8,9},{9,8},{10,11... | collective-permute-start | bytes 1966088 | tf_op jit(solution)/shard_map/ppermute | solution.py:38
  56.1 12.3 %collective-permute-start.6 = (bf16[1024,512]{1,0:T(8,128)(2,1)S(1)}, bf16[1024,512]{1,0:T(8,128)(2,1)}, u32[]{:S(2)}, u32[]{:S(2)}) collective-permute-start(bf16[1024,512]{1,0:T(8,128)(2,1)S(1)} %constant_dynamic-slice_fusion.1), channel_id=1, source_target_pairs={{0,2},{4,6},{8,10},{12,14},{16,18},{20,22},{24,26},{28,30},{33,35}... | collective-permute-start | bytes 3145736 | tf_op jit(solution)/shard_map/ppermute | solution.py:38
  57.9 13.4 %collective-permute-start.9 = (f32[1,64]{1,0:T(1,128)S(1)}, f32[1,64]{1,0:T(1,128)S(1)}, u32[]{:S(2)}, u32[]{:S(2)}) collective-permute-start(f32[1,64]{1,0:T(1,128)S(1)} %bitcast.141), channel_id=1, source_target_pairs={{0,2},{1,3},{2,0},{3,1},{4,6},{5,7},{6,4},{7,5},{8,10},{9,11},{10,... | collective-permute-start | bytes 776 | tf_op jit(solution)/shard_map/ppermute | solution.py:38
  58.1 41.5 %all-to-all-start.1 = ((bf16[16,64,1280]{2,1,0:T(8,128)(2,1)}), bf16[16,64,1280]{2,1,0:T(8,128)(2,1)}, u32[]{:S(2)}, u32[]{:S(2)}) async-start(bf16[16,64,1280]{2,1,0:T(8,128)(2,1)} %bitcast.122), calls=%async_computation.1 | async-start | bytes 5242880 | tf_op jit(solution)/shard_map/all_to_all | solution.py:66
  66.6 23.7 %collective-permute-start.5 = (bf16[1024,512]{1,0:T(8,128)(2,1)}, bf16[1024,512]{1,0:T(8,128)(2,1)}, u32[]{:S(2)}, u32[]{:S(2)}) collective-permute-start(bf16[1024,512]{1,0:T(8,128)(2,1)} %get-tuple-element.29), channel_id=1, source_target_pairs={{0,6},{1,7},{2,4},{3,5},{4,2},{5,3},{6,0},{7,1},{8,14},{9,15},{10,... | collective-permute-start | bytes 3145736 | tf_op jit(solution)/shard_map/ppermute | solution.py:38
  69.8 23.2 %collective-permute-start.7 = (bf16[1024,512]{1,0:T(8,128)(2,1)S(1)}, bf16[1024,512]{1,0:T(8,128)(2,1)}, u32[]{:S(2)}, u32[]{:S(2)}) collective-permute-start(bf16[1024,512]{1,0:T(8,128)(2,1)S(1)} %broadcast_select_fusion.1), channel_id=1, source_target_pairs={{0,1},{2,3},{4,5},{6,7},{8,9},{10,11},{12,13},{14,15},{16,17},{18,... | collective-permute-start | bytes 3145736 | tf_op jit(solution)/shard_map/ppermute | solution.py:38
  102.7 7.3 %collective-permute-start.8 = (bf16[64,1280]{1,0:T(8,128)(2,1)S(1)}, bf16[64,1280]{1,0:T(8,128)(2,1)S(1)}, u32[]{:S(2)}, u32[]{:S(2)}) collective-permute-start(bf16[64,1280]{1,0:T(8,128)(2,1)S(1)} %reduce_sum.39.refs_0_), channel_id=1, source_target_pairs={{4,2},{5,3},{6,0},{7,1},{12,10},{13,11},{14,8},{15,9},{20,18},{21,... | collective-permute-start | bytes 491528 | tf_op jit(solution)/shard_map/ppermute | solution.py:38
  111.9 5.6 %collective-permute-start.11 = (bf16[8,64,128]{2,1,0:T(8,128)(2,1)S(1)}, bf16[8,64,128]{2,1,0:T(8,128)(2,1)S(1)}, u32[]{:S(2)}, u32[]{:S(2)}) collective-permute-start(bf16[8,64,128]{2,1,0:T(8,128)(2,1)S(1)} %shard_map.129.refs_0_), channel_id=1, source_target_pairs={{0,6},{1,7},{2,4},{3,5},{8,14},{9,15},{10,12},{11,13},{16,22},{17,... | collective-permute-start | bytes 393224 | tf_op jit(solution)/shard_map/ppermute | solution.py:38
  119.5 34.5 %all-to-all-start.2 = ((bf16[16,576,128]{2,1,0:T(8,128)(2,1)}), bf16[16,576,128]{2,1,0:T(8,128)(2,1)}, u32[]{:S(2)}, u32[]{:S(2)}) async-start(bf16[16,576,128]{2,1,0:T(8,128)(2,1)} %broadcast_in_dim.86), calls=%async_computation.2 | async-start | bytes 4718592 | tf_op jit(solution)/shard_map/all_to_all | solution.py:66
  157.8 10.4 %collective-permute-start.12 = (bf16[512,512]{1,0:T(8,128)(2,1)}, bf16[512,512]{1,0:T(8,128)(2,1)S(1)}, u32[]{:S(2)}, u32[]{:S(2)}) collective-permute-start(bf16[512,512]{1,0:T(8,128)(2,1)} %shard_map.132), channel_id=1, source_target_pairs={{0,1},{1,0},{2,3},{3,2},{4,5},{5,4},{6,7},{7,6},{8,9},{9,8},{10,11... | collective-permute-start | bytes 1572872 | tf_op jit(solution)/shard_map/ppermute | solution.py:38
  170.1 6.9 %collective-permute-start.13 = (bf16[128,512]{1,0:T(8,128)(2,1)}, bf16[128,512]{1,0:T(8,128)(2,1)}, u32[]{:S(2)}, u32[]{:S(2)}) collective-permute-start(bf16[128,512]{1,0:T(8,128)(2,1)} %get-tuple-element.56), channel_id=1, source_target_pairs={{0,4},{1,5},{2,6},{3,7},{4,0},{5,1},{6,2},{7,3},{8,12},{9,13},{10,... | collective-permute-start | bytes 393224 | tf_op jit(solution)/shard_map/ppermute | solution.py:38
  172.0 9.0 %collective-permute-start.15 = (bf16[128,512]{1,0:T(8,128)(2,1)}, bf16[128,512]{1,0:T(8,128)(2,1)}, u32[]{:S(2)}, u32[]{:S(2)}) collective-permute-start(bf16[128,512]{1,0:T(8,128)(2,1)} %get-tuple-element.57), channel_id=1, source_target_pairs={{0,6},{1,7},{2,0},{3,1},{4,2},{5,3},{6,4},{7,5},{8,14},{9,15},{10,... | collective-permute-start | bytes 393224 | tf_op jit(solution)/shard_map/ppermute | solution.py:38
  173.6 7.4 %collective-permute-start.14 = (bf16[128,512]{1,0:T(8,128)(2,1)}, bf16[128,512]{1,0:T(8,128)(2,1)}, u32[]{:S(2)}, u32[]{:S(2)}) collective-permute-start(bf16[128,512]{1,0:T(8,128)(2,1)} %get-tuple-element.58), channel_id=1, source_target_pairs={{0,2},{1,3},{2,4},{3,5},{4,6},{5,7},{6,0},{7,1},{8,10},{9,11},{10,... | collective-permute-start | bytes 393224 | tf_op jit(solution)/shard_map/ppermute | solution.py:38
  237.9 6.7 %collective-permute-start.17 = (bf16[64,1280]{1,0:T(8,128)(2,1)S(1)}, bf16[64,1280]{1,0:T(8,128)(2,1)S(1)}, u32[]{:S(2)}, u32[]{:S(2)}) collective-permute-start(bf16[64,1280]{1,0:T(8,128)(2,1)S(1)} %bitcast.119), channel_id=1, source_target_pairs={{0,6},{1,7},{2,4},{3,5},{8,14},{9,15},{10,12},{11,13},{16,22},{17,... | collective-permute-start | bytes 491528 | tf_op jit(solution)/shard_map/ppermute | solution.py:38
  246.6 6.9 %collective-permute-start.18 = (bf16[8,64,128]{2,1,0:T(8,128)(2,1)S(1)}, bf16[8,64,128]{2,1,0:T(8,128)(2,1)S(1)}, u32[]{:S(2)}, u32[]{:S(2)}) collective-permute-start(bf16[8,64,128]{2,1,0:T(8,128)(2,1)S(1)} %shard_map.136.refs_0_), channel_id=1, source_target_pairs={{4,2},{5,3},{6,0},{7,1},{12,10},{13,11},{14,8},{15,9},{20,18},{21,... | collective-permute-start | bytes 393224 | tf_op jit(solution)/shard_map/ppermute | solution.py:38
  292.5 6.3 %collective-permute-start.20 = (bf16[128,512]{1,0:T(8,128)(2,1)S(1)}, bf16[128,512]{1,0:T(8,128)(2,1)S(1)}, u32[]{:S(2)}, u32[]{:S(2)}) collective-permute-start(bf16[128,512]{1,0:T(8,128)(2,1)S(1)} %get-tuple-element.51), channel_id=1, source_target_pairs={{0,4},{1,5},{2,6},{3,7},{4,0},{5,1},{6,2},{7,3},{8,12},{9,13},{10,... | collective-permute-start | bytes 393224 | tf_op jit(solution)/shard_map/ppermute | solution.py:38
  292.6 6.3 %collective-permute-start.22 = (bf16[128,512]{1,0:T(8,128)(2,1)S(1)}, bf16[128,512]{1,0:T(8,128)(2,1)S(1)}, u32[]{:S(2)}, u32[]{:S(2)}) collective-permute-start(bf16[128,512]{1,0:T(8,128)(2,1)S(1)} %get-tuple-element.52), channel_id=1, source_target_pairs={{0,6},{1,7},{2,0},{3,1},{4,2},{5,3},{6,4},{7,5},{8,14},{9,15},{10,... | collective-permute-start | bytes 393224 | tf_op jit(solution)/shard_map/ppermute | solution.py:38
  293.1 9.2 %collective-permute-start.21 = (bf16[128,512]{1,0:T(8,128)(2,1)S(1)}, bf16[128,512]{1,0:T(8,128)(2,1)S(1)}, u32[]{:S(2)}, u32[]{:S(2)}) collective-permute-start(bf16[128,512]{1,0:T(8,128)(2,1)S(1)} %get-tuple-element.53), channel_id=1, source_target_pairs={{0,2},{1,3},{2,4},{3,5},{4,6},{5,7},{6,0},{7,1},{8,10},{9,11},{10,... | collective-permute-start | bytes 393224 | tf_op jit(solution)/shard_map/ppermute | solution.py:38
  303.3 10.1 %collective-permute-start.25 = (bf16[32,512]{1,0:T(8,128)(2,1)S(1)}, bf16[32,512]{1,0:T(8,128)(2,1)S(1)}, u32[]{:S(2)}, u32[]{:S(2)}) collective-permute-start(bf16[32,512]{1,0:T(8,128)(2,1)S(1)} %get-tuple-element.77), channel_id=1, source_target_pairs={{0,8},{1,72},{2,24},{3,88},{4,40},{5,104},{6,56},{7,120},{8,0},{9,... | collective-permute-start | bytes 98312 | tf_op jit(solution)/shard_map/ppermute | solution.py:38
  304.4 9.0 %collective-permute-start.26 = (bf16[32,512]{1,0:T(8,128)(2,1)S(1)}, bf16[32,512]{1,0:T(8,128)(2,1)S(1)}, u32[]{:S(2)}, u32[]{:S(2)}) collective-permute-start(bf16[32,512]{1,0:T(8,128)(2,1)S(1)} %get-tuple-element.78), channel_id=1, source_target_pairs={{0,0},{1,64},{2,16},{3,80},{4,32},{5,96},{6,48},{7,112},{8,8},{9,7... | collective-permute-start | bytes 98312 | tf_op jit(solution)/shard_map/ppermute | solution.py:38
  307.2 7.8 %collective-permute-start.24 = (bf16[32,512]{1,0:T(8,128)(2,1)S(1)}, bf16[32,512]{1,0:T(8,128)(2,1)S(1)}, u32[]{:S(2)}, u32[]{:S(2)}) collective-permute-start(bf16[32,512]{1,0:T(8,128)(2,1)S(1)} %get-tuple-element.79), channel_id=1, source_target_pairs={{0,4},{1,68},{2,20},{3,84},{4,36},{5,100},{6,52},{7,116},{8,12},{9... | collective-permute-start | bytes 98312 | tf_op jit(solution)/shard_map/ppermute | solution.py:38
  (36 other events, 267.7 us)
